TPU v7x, 32 devices: a whole 2x2x4 slice. The times are simulated.
32 devices in a mesh: groups: 1, slab: 4 (over z), sub: 4 (over y, x), chan: 2 (over core).
Axes of the slice: x: 2, y: 2, z: 4, core: 2. Of those that a mesh axis runs over, the one named last changes fastest.
Arguments:
- coords: float32 [3, 16384], P(None, ('groups', 'slab', 'sub')), may hold values from 0 to 128
- features: bfloat16 [16384, 64], P(('groups', 'slab', 'sub'), 'chan'), may hold values from -6 to 6
- valid_count: int32 [128], P(('groups', 'slab', 'sub')), may hold values from 1 to 128
- pair_block: int32 [4, 4, 4, 4], P(('groups', 'slab')), may hold values from 0 to 7, as said below
- pair_brick: int32 [4, 4, 4, 4], P(('groups', 'slab')), may hold values from 0 to 16383, as said below
- pair_count: int32 [4, 4, 4], P(('groups', 'slab')), may hold values from 0 to 4, as said below
- geometry: bfloat16 [64, 128, 128, 128], P('chan', ('groups', 'slab', 'sub')), may hold values from -6 to 6
- encoder_first: float32 [3, 64], replicated, may hold values from -3.5 to 3.5
- encoder_bias: float32 [64], replicated, may hold values from -3 to 3
- encoder_second: float32 [64, 64], P(None, 'chan'), may hold values from -0.75 to 0.75
- decoder_first: float32 [3, 64], replicated, may hold values from -3.5 to 3.5
- decoder_bias: float32 [64], replicated, may hold values from -3 to 3
- decoder_second: float32 [64, 64], P(None, 'chan'), may hold values from -0.75 to 0.75
- spectral: bfloat16 [1024, 32, 64, 64], P(('slab', 'sub')), may hold values from -4.1875 to 4.1875
- cotangent: bfloat16 [16384, 64], P(('groups', 'slab', 'sub'), 'chan'), may hold values from -6 to 6
Outputs:
- decoded: bfloat16 [16384, 64], P(('groups', 'slab', 'sub'), 'chan')
- grad_encoder_first: float32 [3, 64], P('groups')
- grad_encoder_bias: float32 [64], P('groups')
- grad_encoder_second: float32 [64, 64], P('groups', 'chan')
- grad_decoder_first: float32 [3, 64], P('groups')
- grad_decoder_bias: float32 [64], P('groups')
- grad_decoder_second: float32 [64, 64], P('groups', 'chan')
- grad_spectral: bfloat16 [1024, 32, 64, 64], P(('groups', 'slab', 'sub'), None, 'chan')
Inputs may be any that keep to these rules, and one draw needn't show every extreme that they name: `pair_block`: a point block of the source device. `pair_brick`: a grid block of the destination device. Slot r to destination d is live if r < pair_count; in every draw some device receives 4 live slots from every device of its slab.
All inputs are finite; a program needn't handle non-finite values.
Results may differ from a plain program's by a relative error of at most 0.0045.
Values may be sent and summed in bfloat16 or wider, within the bound.
No kernel may reach another device: no remote copies, remote signals or barrier semaphores. Data moves between devices by JAX's collectives and lax.ppermute only.
A program may use at most 320 MiB of HBM per device.

v0:
```python
import functools

import jax
import jax.numpy as jnp
import numpy as np
from jax import lax
from jax.experimental import pallas as pl
from jax.experimental.pallas import tpu as pltpu
from jax.sharding import PartitionSpec as P

MODES = 32
BLOCK = 128
BRICK = 8
CAP = 4
RADIUS = 4.0
QUADRATURE = 0.0625
ROWS = 48

F32 = jnp.float32
BF16 = jnp.bfloat16
MIB = 1 << 20

NN = (((1,), (0,)), ((), ()))
NT = (((1,), (1,)), ((), ()))
TN = (((0,), (0,)), ((), ()))


def dot(a, b, dims=NN):
    return lax.dot_general(a, b, dims, preferred_element_type=F32)


def raw_basis(length):
    half = MODES // 2
    n = np.arange(length)[:, None]
    m = np.arange(half)[None, :]
    values = np.concatenate(
        [np.cos(2 * np.pi * m * n / length), np.sin(2 * np.pi * (m + 1) * n / length)], axis=1
    )
    norm = np.full(MODES, np.sqrt(2.0 / length))
    norm[0] = np.sqrt(1.0 / length)
    return values, norm


def halves(values):
    high = np.asarray(values, np.float32).astype(jnp.bfloat16)
    low = (np.asarray(values, np.float64) - high.astype(np.float64)).astype(jnp.bfloat16)
    return high, low


def split(value):
    high = value.astype(BF16).astype(F32)
    return high, value - high


def gelu_pair(x):
    a = 0.7978845608028654
    b = a * 0.044715
    x2 = x * x
    t = jnp.tanh(x * (a + b * x2))
    half = 0.5 + 0.5 * t
    slope = half + (0.5 * x) * (1.0 - t * t) * (a + (3.0 * b) * x2)
    return x * half, slope


def smem():
    return pl.BlockSpec(memory_space=pltpu.SMEM)


def vmem():
    return pl.BlockSpec(memory_space=pltpu.VMEM)


def params(mib):
    return pltpu.CompilerParams(vmem_limit_bytes=mib * MIB)


def cost(flops, nbytes):
    return pl.CostEstimate(flops=int(flops), bytes_accessed=int(nbytes), transcendentals=0)


def slot_offsets(s, cell, xs):
    return [cell[d, s] - xs[d : d + 1, :] for d in range(3)]


def slot_mask(s, b, live, count, weight):
    lanes = lax.broadcasted_iota(jnp.int32, (1, BLOCK), 1)
    return jnp.where(lanes < count[b], weight, 0.0) * live[s]


def net_kernel(
    sign, weight, keep, slots, blk, cell, live, count, x_ref, f_ref, w1_ref, w2_ref, *rest
):
    if keep:
        g_ref, slope_ref, part_ref, hid_all, part = rest
    else:
        crow_ref, g_ref, slope_ref, part_ref, hid_all, part = rest
    chan = f_ref.shape[0]
    hidden = w2_ref.shape[0]
    wide = BRICK * hidden
    part[...] = jnp.zeros_like(part)

    def step(s, carry):
        b = blk[s]
        at = pl.multiple_of(b * BLOCK, BLOCK)
        xs = x_ref[:, pl.ds(at, BLOCK)]
        mask = slot_mask(s, b, live, count, weight)
        f = (f_ref[:, pl.ds(at, BLOCK)].astype(F32) * mask).astype(BF16)
        e = slot_offsets(s, cell, xs)
        base = w1_ref[0] * e[0] + w1_ref[1] * e[1] + w1_ref[2] * e[2]
        base = w1_ref[3] + sign * base
        row = pl.multiple_of(s * wide, wide)
        hrow = row if keep else 0
        for q in range(BRICK):
            value, slope = gelu_pair(base + (sign * q) * w1_ref[2])
            hid_all[pl.ds(hrow + q * hidden, hidden), :] = value.astype(BF16)
            slope_ref[pl.ds(row + q * hidden, hidden), :] = slope.astype(BF16)
        g = dot(hid_all[pl.ds(hrow, wide), :], f, NT)
        g_ref[pl.ds(row, wide), :] = g.astype(BF16)
        summed = jnp.sum(g.reshape(BRICK, hidden, chan) * w2_ref[...][None], axis=1)
        part[pl.ds(pl.multiple_of(s * BRICK, BRICK), BRICK), 0:chan] = summed
        return carry

    lax.fori_loop(0, slots, step, 0)
    turned = jnp.transpose(part[...])[0:chan, :]
    if keep:
        part_ref[...] = turned
    else:
        message = jnp.concatenate([turned, crow_ref[...]], axis=0).astype(BF16)

        def copy(i, carry):
            part_ref[i] = message
            return carry

        lax.fori_loop(0, part_ref.shape[0], copy, 0)


def back_kernel(sign, weight, decode, slots, blk, cell, live, count, *rest):
    if decode:
        (x_ref, f_ref, w1_ref, w2_ref, g_ref, slope_ref, gp_ref, hid_ref,
         out_ref, dec_ref, m_ref, turn, dec) = rest
        gp = gp_ref[...]
        dec[...] = jnp.zeros_like(dec)
    else:
        x_ref, f_ref, w1_ref, w2_ref, g_ref, slope_ref, own_ref, recv_ref, out_ref, m_ref, turn = rest
        gp = own_ref[...] + jnp.sum(recv_ref[...].astype(F32), axis=0)
    chan = f_ref.shape[0]
    hidden = w2_ref.shape[0]
    wide = BRICK * hidden
    cells = gp.shape[1]
    turn[...] = jnp.transpose(
        jnp.concatenate([gp, jnp.zeros((128 - chan, cells), F32)], axis=0)
    )

    def step(s, carry):
        acc, grad2 = carry
        b = blk[s]
        at = pl.multiple_of(b * BLOCK, BLOCK)
        xs = x_ref[:, pl.ds(at, BLOCK)]
        mask = slot_mask(s, b, live, count, weight)
        f = (f_ref[:, pl.ds(at, BLOCK)].astype(F32) * mask).astype(BF16)
        e = slot_offsets(s, cell, xs)
        row = pl.multiple_of(s * wide, wide)
        gps = turn[pl.ds(pl.multiple_of(s * BRICK, BRICK), BRICK), 0:chan]
        for q in range(BRICK):
            line = gps[q : q + 1, :]
            m_ref[q * hidden : (q + 1) * hidden, :] = (w2_ref[...] * line).astype(BF16)
            grad2 = grad2 + line * g_ref[pl.ds(row + q * hidden, hidden), :].astype(F32)
        back = dot(m_ref[...], f)
        sum0 = jnp.zeros((hidden, BLOCK), F32)
        sum1 = jnp.zeros((hidden, BLOCK), F32)
        for q in range(BRICK):
            value = back[q * hidden : (q + 1) * hidden, :] * slope_ref[
                pl.ds(row + q * hidden, hidden), :
            ].astype(F32)
            sum0 = sum0 + value
            if q:
                sum1 = sum1 + float(q) * value
        scale = sign / RADIUS
        acc = (
            acc[0] + sum0 * (e[0] * scale),
            acc[1] + sum0 * (e[1] * scale),
            acc[2] + (sum0 * (e[2] * scale) + sum1 * scale),
            acc[3] + sum0,
        )
        if decode:
            inside = slot_mask(s, b, live, count, 1.0 / BRICK)
            value = dot(m_ref[...], hid_ref[pl.ds(row, wide), :], TN)
            dec[b] = dec[b] + value * inside
        return acc, grad2

    zero = jnp.zeros((hidden, BLOCK), F32)
    acc, grad2 = lax.fori_loop(
        0, slots, step, ((zero,) * 4, jnp.zeros((hidden, chan), F32))
    )
    sums = [jnp.sum(a, axis=1, keepdims=True) for a in acc]
    packed = jnp.concatenate(
        [grad2] + sums + [jnp.zeros((hidden, 128 - chan - 4), F32)], axis=1
    )
    out_ref[...] = jnp.transpose(packed)[0 : chan + 8, :]
    if decode:
        for b in range(dec.shape[0]):
            dec_ref[:, b * BLOCK : (b + 1) * BLOCK] = dec[b].astype(BF16)


def dense_kernel(planes, me, held, x_ref, fk_ref, lh_ref, ll_ref, perm_ref, out_ref, gb_ref, th, tl):
    p = pl.program_id(0)
    chan = x_ref.shape[0]
    length = x_ref.shape[2]
    for group in range(chan // 4):
        a = jnp.concatenate([x_ref[4 * group + i, 0] for i in range(4)], axis=1)
        t = dot(a, fk_ref[...])
        high, low = split(t[:, 0:128] + t[:, 128:256])
        rows = pl.ds(pl.multiple_of(p * length, length), length)
        th[rows, group * 128 : (group + 1) * 128] = high.astype(BF16)
        tl[rows, group * 128 : (group + 1) * 128] = low.astype(BF16)

    @pl.when(p == 0)
    def _():
        gb_ref[...] = jnp.zeros_like(gb_ref)

    cells = gb_ref.shape[2]

    def slot(t, carry):
        @pl.when(held[0, t] == p)
        def _():
            row = held[1, t]
            first = pl.multiple_of((row // 16) * 16, 16)
            tile = x_ref[:, 0, pl.ds(first, 16), :].astype(F32)
            inside = lax.broadcasted_iota(jnp.int32, (1, 16, 128), 1) == row - first
            line = jnp.sum(jnp.where(inside, tile, 0.0), axis=1).astype(BF16)
            u = t // CAP
            begin = (me[0] * CAP + t % CAP) * BRICK
            k = lax.broadcasted_iota(jnp.int32, (128, cells), 0)
            lane = lax.broadcasted_iota(jnp.int32, (128, cells), 1) - begin
            hot = (k == held[2, t] * BRICK + lane) & (lane >= 0) & (lane < BRICK)
            picked = dot(line, jnp.where(hot, 1.0, 0.0).astype(BF16))
            gb_ref[u] = gb_ref[u] + picked.astype(BF16)

        return carry

    lax.fori_loop(0, held.shape[1], slot, 0)

    @pl.when(p == planes - 1)
    def _():
        for piece in range(2):
            cols = slice(piece * 512, (piece + 1) * 512)
            r = dot(lh_ref[...], th[:, cols]) + dot(lh_ref[...], tl[:, cols])
            r = (r + dot(ll_ref[...], th[:, cols])).astype(BF16)
            th[0 : r.shape[0], cols] = r
        rows = out_ref.shape[0]
        out_ref[...] = dot(th[0:rows, :], perm_ref[...]).astype(BF16)


def prep_kernel(
    where, ag_ref, kx_ref, ix_ref, fj_ref, scale_ref, id_ref, gown_ref,
    bt_ref, dcoef_ref, lat_ref, p_ref,
):
    cells = ag_ref.shape[3]
    devices = ag_ref.shape[1]
    chan = p_ref.shape[0] // 2
    rows = bt_ref.shape[0]
    per = max(1, 256 // cells)
    width = per * cells
    piece = min(rows, 256)

    def place(i, carry):
        parts = [ag_ref[0, i * per + j, chan:ROWS, :].astype(F32) for j in range(per)]
        lines = jnp.concatenate(parts, axis=1)
        iota = lax.broadcasted_iota(jnp.int32, (128, width), 0).astype(F32)

        def hot(r):
            one = jnp.where(iota == lines[r : r + 1, :], 1.0, 0.0).astype(BF16)
            return jnp.concatenate([one, one], axis=0)

        tj = dot(fj_ref[...], hot(1))[0:1, :]
        hi, hk = hot(0), hot(2)
        at = pl.ds(pl.multiple_of(i * width, width), width)
        for r in range(rows // piece):
            rs = slice(r * piece, (r + 1) * piece)
            value = dot(kx_ref[rs, :], hk) * (dot(ix_ref[rs, :], hi) * tj)
            bt_ref[rs, at] = value.astype(BF16)
        for j in range(per):
            here = pl.ds(pl.multiple_of(i * width + j * cells, cells), cells)
            for c in range(2):
                p_ref[c * chan : (c + 1) * chan, here] = ag_ref[c, i * per + j, 0:chan, :]
        return carry

    lax.fori_loop(0, devices // per, place, 0)
    dcoef_ref[...] = dot(bt_ref[...], p_ref[...], NT) * scale_ref[...]
    subs = gown_ref.shape[0]
    encoded = jnp.zeros(lat_ref.shape, F32)
    for u in range(subs):
        lines = ag_ref[0, where[0] + u, chan:ROWS, :].astype(F32)
        same = cell_number(lines) == id_ref[...]
        here = ag_ref[where[1], where[0] + u, 0:chan, :]
        encoded = encoded + dot(here, jnp.where(same, 1.0, 0.0).astype(BF16), NT)
    geometry = jnp.sum(gown_ref[...].astype(F32), axis=0)
    lat_ref[...] = (geometry + encoded).astype(BF16).astype(F32)


def cell_number(lines):
    return lines[0:1, :] * 16384.0 + lines[1:2, :] * 128.0 + lines[2:3, :]


def send_cells(modes_rows, scale_row, bt_ref, sy_ref, turned):
    rows, devices2, chan, cells = bt_ref.shape[0], sy_ref.shape[0], sy_ref.shape[1], sy_ref.shape[2]
    value = jnp.transpose(modes_rows)[0 : 2 * chan, :] * scale_row
    high, low = split(value)
    turned[...] = jnp.concatenate([high, low], axis=0).astype(BF16)
    per = max(1, 256 // cells)
    width = per * cells

    def step(i, carry):
        at = pl.ds(pl.multiple_of(i * width, width), width)
        o = dot(turned[...], bt_ref[:, at])
        o = (o[0 : 2 * chan] + o[2 * chan :]).astype(BF16)
        for j in range(per):
            for c in range(2):
                sy_ref[(i * per + j) * 2 + c] = o[
                    c * chan : (c + 1) * chan, j * cells : (j + 1) * cells
                ]
        return carry

    lax.fori_loop(0, devices2 // 2 // per, step, 0, unroll=2)


def eight_mask():
    lane = lax.broadcasted_iota(jnp.int32, (8, 512), 1) // 64
    return jnp.where(lane == lax.broadcasted_iota(jnp.int32, (8, 512), 0), 1.0, 0.0)


def mix_kernel(
    chan_index, recv_ref, fi_ref, dcoef_ref, w_ref, bt_ref, scale_ref,
    sy_ref, coef_ref, coef, mix, turned,
):
    step = pl.program_id(0)
    steps = pl.num_programs(0)
    number = coef.shape[0] // MODES
    chan = coef_ref.shape[0] // 2

    @pl.when(step == 0)
    def _():
        mix[...] = jnp.zeros_like(mix)
        for c in range(2):
            if len(recv_ref.shape) == 4:
                got = recv_ref[:, c].astype(F32)
                got = got.reshape(got.shape[0] * got.shape[1], got.shape[2]).astype(BF16)
            else:
                got = recv_ref[c]
            x = dot(fi_ref[...], got)
            x = x[0:MODES] + x[MODES:]
            for n in range(number):
                coef[n * MODES : (n + 1) * MODES, c * chan : (c + 1) * chan] = x[
                    :, n * chan : (n + 1) * chan
                ]
        full = coef[:, 0 : 2 * chan] + dcoef_ref[...]
        coef[:, 0 : 2 * chan] = full
        coef[:, 2 * chan :] = jnp.zeros((coef.shape[0], 128 - 2 * chan), F32)
        coef_ref[...] = jnp.transpose(coef[...])[0 : 2 * chan, :]

    mask = eight_mask()
    here = w_ref.shape[0]
    for nn in range(here):
        for group in range(MODES // 8):
            rows = pl.ds(pl.multiple_of((step * here + nn) * MODES + group * 8, 8), 8)
            c8 = coef[rows, 0:64]
            c128 = jnp.concatenate([c8, c8], axis=1)
            big = jnp.concatenate([c128] * 4, axis=1) * mask
            high, low = split(big)
            left = jnp.concatenate([high, low], axis=0).astype(BF16)
            right = w_ref[nn, group * 8 : (group + 1) * 8].reshape(512, 64)
            o = dot(left, right)
            mix[rows, 0:64] = o[0:8] + o[8:16]

    @pl.when(step == steps - 1)
    def _():
        send_cells(mix[...], scale_ref[...], bt_ref, sy_ref, turned)


def mixback_kernel(
    chan_index, recv_ref, w_ref, bt_ref, column_ref, scale_ref,
    sy_ref, gm_ref, gm, mix, turned, g_ref,
):
    step = pl.program_id(0)
    steps = pl.num_programs(0)
    devices2, chan, cells = recv_ref.shape

    @pl.when(step == 0)
    def _():
        mix[...] = jnp.zeros_like(mix)
        gm[...] = jnp.zeros_like(gm)

        def place(i, carry):
            at = pl.ds(pl.multiple_of(i * cells, cells), cells)
            for c in range(2):
                g_ref[c * chan : (c + 1) * chan, at] = recv_ref[2 * i + c]
            return carry

        lax.fori_loop(0, devices2 // 2, place, 0)
        gm[:, 0:64] = dot(bt_ref[...], g_ref[...], NT) * column_ref[...]
        gm_ref[...] = jnp.transpose(gm[...])[0:64, :]

    mask = eight_mask()
    here = w_ref.shape[0]
    for nn in range(here):
        for group in range(MODES // 8):
            rows = pl.ds(pl.multiple_of((step * here + nn) * MODES + group * 8, 8), 8)
            high, low = split(gm[rows, 0:64])
            left = jnp.concatenate([high, low], axis=0).astype(BF16)
            right = w_ref[nn, group * 8 : (group + 1) * 8].reshape(512, 64)
            o = dot(left, right, NT)
            o = (o[0:8] + o[8:16]) * mask
            o = (o[:, 0:128] + o[:, 128:256]) + (o[:, 256:384] + o[:, 384:512])
            mix[rows, 0:64] = o[:, 0:64] + o[:, 64:128]

    @pl.when(step == steps - 1)
    def _():
        send_cells(mix[...], scale_ref[...], bt_ref, sy_ref, turned)


def point_kernel(recv_ref, lat_ref, rg_ref, g_ref, b_ref):
    preact = lat_ref[...] + jnp.sum(recv_ref[...].astype(F32), axis=0)
    value, slope = gelu_pair(preact)
    b_ref[...] = value.astype(BF16).astype(F32)
    g = (slope * rg_ref[...]).astype(BF16)

    def copy(i, carry):
        g_ref[i] = g
        return carry

    lax.fori_loop(0, g_ref.shape[0], copy, 0)


def own_kernel(where, ag_ref, recv_ref, id_ref, out_ref):
    chan = recv_ref.shape[1]
    total = jnp.zeros(out_ref.shape, F32)
    for u in range(where.shape[0] - 2):
        lines = ag_ref[0, where[0] + u, chan:ROWS, :].astype(F32)
        same = jnp.where(cell_number(lines) == id_ref[...], 1.0, 0.0).astype(BF16)
        total = total + dot(recv_ref[(where[0] + u) * 2 + where[1]], same, NT)
    out_ref[...] = total


def outer_kernel(chan_index, c_own, c_far, g_own, g_far, out_ref):
    mine = pl.program_id(0) == chan_index[0]
    coef = jnp.where(mine, c_own[...], c_far[...])
    grad = jnp.transpose(jnp.where(mine, g_own[...], g_far[...]))
    width = coef.shape[1]
    for x in range(width):
        value = coef[:, x : x + 1] * grad[x : x + 1, :]
        out_ref[x // MODES, x % MODES] = value.astype(BF16)


def tables(planes, devices, count_j, count_k):
    count_i = planes * devices
    raw_i, norm_i = raw_basis(count_i)
    raw_j, norm_j = raw_basis(count_j)
    raw_k, norm_k = raw_basis(count_k)
    fk_high, fk_low = halves(raw_k * norm_k)
    fk = np.zeros((4, count_k, 2, 4, MODES), jnp.bfloat16)
    for c in range(4):
        fk[c, :, 0, c] = fk_high
        fk[c, :, 1, c] = fk_low
    fj_high, fj_low = halves(raw_j * norm_j)
    left = np.zeros((2, MODES, planes, planes, count_j), jnp.bfloat16)
    for p in range(planes):
        left[0, :, p, p] = fj_high.T
        left[1, :, p, p] = fj_low.T
    left = left.reshape(2, MODES * planes, planes * count_j)
    fi_high, fi_low = halves(raw_i * norm_i)
    fi = np.concatenate([fi_high.T, fi_low.T], axis=0)

    def expand(raw, order):
        high, low = halves(raw)
        both = np.concatenate([high.T, low.T], axis=1)
        return np.repeat(both, MODES, axis=0) if order == "rep" else np.tile(both, (MODES, 1))

    kx = expand(raw_k, "rep")
    ix = expand(raw_i, "tile")
    fj_rows = np.concatenate([h.T for h in halves(raw_j)], axis=1)
    norm_nl = np.repeat(norm_k, MODES) * np.tile(norm_i, MODES)
    return {
        "fk": fk.reshape(4 * count_k, 8 * MODES),
        "lh": left[0],
        "ll": left[1],
        "fi": fi,
        "kx": kx,
        "ix": ix,
        "fj": fj_rows,
        "norm_nl": norm_nl.astype(np.float32),
        "norm_j": norm_j.astype(np.float32),
    }


def permutation(chan):
    perm = np.zeros((chan, MODES, MODES, chan), jnp.bfloat16)
    for c in range(chan):
        for n in range(MODES):
            perm[c, n, n, c] = 1
    return perm.reshape(chan * MODES, MODES * chan)


def body(
    coords,
    features,
    valid_count,
    pair_block,
    pair_brick,
    pair_count,
    geometry,
    encoder_first,
    encoder_bias,
    encoder_second,
    decoder_first,
    decoder_bias,
    decoder_second,
    spectral,
    cotangent,
):
    subs = lax.axis_size("sub")
    devices = lax.axis_size("slab") * subs
    every = ("slab", "sub", "chan")
    slab_index = lax.axis_index("slab")
    sub_index = lax.axis_index("sub")
    chan_index = lax.axis_index("chan")
    pair = slab_index * subs + sub_index
    blocks_here = valid_count.shape[0]
    chan, planes, count_j, count_k = geometry.shape
    points = features.shape[0]
    hidden = encoder_first.shape[1]
    slots = subs * CAP
    cells = slots * BRICK
    all_cells = devices * cells
    own = spectral.shape[0] // 2
    rows = own * MODES
    split_n = MODES // own
    tab = tables(planes, devices, count_j, count_k)
    per_row = count_k // BRICK

    blk = lax.dynamic_index_in_dim(pair_block[0], sub_index, 0, keepdims=False).reshape(slots)
    brick = lax.dynamic_index_in_dim(pair_brick[0], sub_index, 0, keepdims=False).reshape(slots)
    limits = lax.dynamic_index_in_dim(pair_count[0], sub_index, 0, keepdims=False)
    number = jnp.arange(slots, dtype=jnp.int32)
    target = number // CAP
    live = (number % CAP < jnp.repeat(limits, CAP)).astype(F32)

    def place(values):
        return values // (count_j * per_row), values // per_row % count_j, values % per_row

    layer, row, column = place(brick)
    plane = (slab_index * subs + target) * planes + layer
    cell = jnp.stack([plane, row, column * BRICK]).astype(F32) + 0.5
    lane_i = jnp.repeat(plane, BRICK)
    lane_j = jnp.repeat(row, BRICK)
    lane_k = jnp.repeat(column * BRICK, BRICK) + jnp.tile(jnp.arange(BRICK, dtype=jnp.int32), slots)
    coordinate_rows = jnp.concatenate(
        [jnp.stack([lane_i, lane_j, lane_k]).astype(F32), jnp.zeros((ROWS - chan - 3, cells), F32)]
    )
    own_id = (lane_i * 16384 + lane_j * 128 + lane_k).astype(F32)[:, None]
    held_brick = lax.dynamic_index_in_dim(pair_brick[0], sub_index, 1, keepdims=False).reshape(slots)
    held = jnp.stack(place(held_brick))
    where = jnp.concatenate(
        [jnp.stack([slab_index * subs, chan_index]), jnp.zeros((subs,), jnp.int32)]
    ).astype(jnp.int32)
    me = sub_index.astype(jnp.int32).reshape(1)
    core = chan_index.astype(jnp.int32).reshape(1)

    def first_layer(first, bias):
        stacked = jnp.concatenate([first / RADIUS, bias[None]], axis=0)
        return jnp.broadcast_to(stacked[:, :, None], (4, hidden, BLOCK))

    enc_w1 = first_layer(encoder_first, encoder_bias)
    dec_w1 = first_layer(decoder_first, decoder_bias)
    features_t = features.T
    cotangent_t = cotangent.T
    wide = BRICK * hidden

    def net(sign, weight, keep, f, w1, w2):
        hid_rows = slots * wide if keep else wide
        outs = [
            jax.ShapeDtypeStruct((slots * wide, chan), BF16),
            jax.ShapeDtypeStruct((slots * wide, BLOCK), BF16),
        ]
        args = [blk, cell, live, valid_count, coords, f, w1, w2]
        scratch = [pltpu.VMEM((cells, 128), F32)]
        if keep:
            outs.append(jax.ShapeDtypeStruct((chan, cells), F32))
            outs.append(jax.ShapeDtypeStruct((hid_rows, BLOCK), BF16))
        else:
            outs.append(jax.ShapeDtypeStruct((devices, ROWS, cells), BF16))
            args.append(coordinate_rows)
            scratch = [pltpu.VMEM((wide, BLOCK), BF16)] + scratch
        return pl.pallas_call(
            functools.partial(net_kernel, sign, weight, keep, slots),
            out_shape=outs,
            in_specs=[smem()] * 4 + [vmem()] * (len(args) - 4),
            out_specs=[vmem()] * len(outs),
            scratch_shapes=scratch,
            compiler_params=params(32),
            cost_estimate=cost(2e9, 8e6),
        )(*args)

    with jax.named_scope("encoder_points"):
        enc_g, enc_slope, message = net(
            1.0, QUADRATURE, False, features_t, enc_w1, encoder_second
        )
    with jax.named_scope("partials_all"):
        near = lax.all_to_all(message, ("slab", "sub"), 0, 0, tiled=True)
        gathered = lax.all_gather(near, "chan", axis=0)

    with jax.named_scope("dense_transform"):
        lanes = chan * MODES
        dense, held_values = pl.pallas_call(
            functools.partial(dense_kernel, planes),
            grid=(planes,),
            out_shape=[
                jax.ShapeDtypeStruct((MODES * planes, lanes), BF16),
                jax.ShapeDtypeStruct((subs, chan, cells), BF16),
            ],
            in_specs=[
                smem(),
                smem(),
                pl.BlockSpec((chan, 1, count_j, count_k), lambda p: (0, p, 0, 0)),
            ]
            + [vmem()] * 4,
            out_specs=[
                pl.BlockSpec((MODES * planes, lanes), lambda p: (0, 0)),
                pl.BlockSpec((subs, chan, cells), lambda p: (0, 0, 0)),
            ],
            scratch_shapes=[
                pltpu.VMEM((planes * count_j, lanes), BF16),
                pltpu.VMEM((planes * count_j, lanes), BF16),
            ],
            compiler_params=params(40),
            cost_estimate=cost(8e9, 1e7),
        )(
            me,
            held,
            geometry,
            jnp.asarray(tab["fk"]),
            jnp.asarray(tab["lh"]),
            jnp.asarray(tab["ll"]),
            jnp.asarray(permutation(chan)),
        )
    with jax.named_scope("dense_exchange"):
        dense = dense.reshape(MODES, planes, split_n, own * chan)
        dense = dense.transpose(0, 2, 1, 3).reshape(MODES * split_n, planes, own * chan)
        dense = lax.all_to_all(dense, every, 0, 0, tiled=True)
        dense = dense.reshape(devices, 2, planes, own * chan)
        if planes % 8:
            dense = dense.transpose(1, 0, 2, 3).reshape(2, devices * planes, own * chan)
    with jax.named_scope("held_exchange"):
        geometry_own = lax.all_to_all(held_values, "sub", 0, 0, tiled=True)

    with jax.named_scope("decoder_points"):
        dec_g, dec_slope, read_grads, dec_hid = net(
            -1.0, 1.0 / BRICK, True, cotangent_t, dec_w1, decoder_second
        )

    first_pair = (pair * 2 + chan_index) * own
    mode_j = first_pair // MODES
    kx = jnp.asarray(tab["kx"])
    norm_nl = jnp.asarray(tab["norm_nl"])
    if split_n > 1:
        begin = first_pair % MODES * MODES
        kx = lax.dynamic_slice_in_dim(kx, begin, rows, 0)
        norm_nl = lax.dynamic_slice_in_dim(norm_nl, begin, rows, 0)
    scale = norm_nl * lax.dynamic_index_in_dim(jnp.asarray(tab["norm_j"]), mode_j, 0, keepdims=False)
    scale_column, scale_row = scale[:, None], scale[None, :]
    fj = lax.dynamic_slice_in_dim(jnp.asarray(tab["fj"]), mode_j, 1, 0)
    fj = jnp.broadcast_to(fj, (16, fj.shape[1]))

    with jax.named_scope("cell_basis"):
        bt, sparse_coef, latent = pl.pallas_call(
            prep_kernel,
            out_shape=[
                jax.ShapeDtypeStruct((rows, all_cells), BF16),
                jax.ShapeDtypeStruct((rows, 2 * chan), F32),
                jax.ShapeDtypeStruct((chan, cells), F32),
            ],
            in_specs=[smem()] + [vmem()] * 7,
            out_specs=[vmem()] * 3,
            scratch_shapes=[pltpu.VMEM((2 * chan, all_cells), BF16)],
            compiler_params=params(40),
            cost_estimate=cost(5e9, 8e6),
        )(
            where,
            gathered,
            kx,
            jnp.asarray(tab["ix"][:rows]),
            fj,
            scale_column,
            own_id,
            geometry_own,
        )

    block_n = min(4, own)
    steps = own // block_n

    def weights_spec():
        return pl.BlockSpec(
            (block_n, MODES, 2 * chan, 2 * chan), lambda n, core: (core[0] * steps + n, 0, 0, 0)
        )

    def whole(array):
        rank = len(array.shape)
        return pl.BlockSpec(array.shape, lambda n, core: (0,) * rank)

    def mode_call(kernel, args, outs, scratch):
        specs = [weights_spec() if a is spectral else whole(a) for a in args]
        return pl.pallas_call(
            kernel,
            grid_spec=pltpu.PrefetchScalarGridSpec(
                num_scalar_prefetch=1,
                grid=(steps,),
                in_specs=specs,
                out_specs=[whole(o) for o in outs],
                scratch_shapes=scratch,
            ),
            out_shape=outs,
            compiler_params=params(40),
            cost_estimate=cost(4e9, 2.4e7),
        )(core, *args)

    readers = jax.ShapeDtypeStruct((2 * devices, chan, cells), BF16)
    by_mode = jax.ShapeDtypeStruct((2 * chan, rows), F32)
    with jax.named_scope("mix"):
        sent, coefficient = mode_call(
            mix_kernel,
            [dense, jnp.asarray(tab["fi"]), sparse_coef, spectral, bt, scale_row],
            [readers, by_mode],
            [
                pltpu.VMEM((rows, 128), F32),
                pltpu.VMEM((rows, 128), F32),
                pltpu.VMEM((4 * chan, rows), BF16),
            ],
        )
    with jax.named_scope("preact_exchange"):
        arrived = lax.all_to_all(sent, every, 0, 0, tiled=True)
    swap = [(0, 1), (1, 0)]
    with jax.named_scope("coefficient_swap"):
        coef_near = lax.dynamic_slice_in_dim(coefficient, chan_index * chan, chan, 0)
        coef_sent = lax.dynamic_slice_in_dim(coefficient, (1 - chan_index) * chan, chan, 0)
        coef_far = lax.ppermute(coef_sent, "chan", swap)

    with jax.named_scope("cell_values"):
        cell_grads, bricks = pl.pallas_call(
            point_kernel,
            out_shape=[readers, jax.ShapeDtypeStruct((chan, cells), F32)],
            in_specs=[vmem()] * 3,
            out_specs=[vmem()] * 2,
            compiler_params=params(16),
            cost_estimate=cost(1e6, 1e6),
        )(arrived, latent, read_grads)
    with jax.named_scope("cell_grads_all"):
        all_grads = lax.all_to_all(cell_grads, every, 0, 0, tiled=True)

    def back(sign, weight, decode, f, w1, w2, g, slope, *more):
        args = [blk, cell, live, valid_count, coords, f, w1, w2, g, slope, *more]
        outs = [jax.ShapeDtypeStruct((chan + 8, hidden), F32)]
        scratch = [pltpu.VMEM((wide, chan), BF16), pltpu.VMEM((cells, 128), F32)]
        if decode:
            outs.append(jax.ShapeDtypeStruct((chan, points), BF16))
            scratch.append(pltpu.VMEM((blocks_here, chan, BLOCK), F32))
        return pl.pallas_call(
            functools.partial(back_kernel, sign, weight, decode, slots),
            out_shape=outs,
            in_specs=[smem()] * 4 + [vmem()] * (len(args) - 4),
            out_specs=[vmem()] * len(outs),
            scratch_shapes=scratch,
            compiler_params=params(32),
            cost_estimate=cost(2e9, 8e6),
        )(*args)

    with jax.named_scope("decoder_back"):
        dec_grads, decoded = back(
            -1.0, 1.0 / BRICK, True, cotangent_t, dec_w1, decoder_second,
            dec_g, dec_slope, bricks, dec_hid,
        )

    with jax.named_scope("mix_back"):
        sent_back, grad_modes = mode_call(
            mixback_kernel,
            [all_grads, spectral, bt, scale_column, scale_row],
            [readers, by_mode],
            [
                pltpu.VMEM((rows, 128), F32),
                pltpu.VMEM((rows, 128), F32),
                pltpu.VMEM((4 * chan, rows), BF16),
                pltpu.VMEM((2 * chan, all_cells), BF16),
            ],
        )
    with jax.named_scope("latent_grad_exchange"):
        arrived_back = lax.all_to_all(sent_back, every, 0, 0, tiled=True)
    with jax.named_scope("grad_swap"):
        grad_far = lax.ppermute(grad_modes, "chan", swap)
    with jax.named_scope("own_cells"):
        own_grads = pl.pallas_call(
            own_kernel,
            out_shape=jax.ShapeDtypeStruct((chan, cells), F32),
            in_specs=[smem()] + [vmem()] * 3,
            out_specs=vmem(),
            compiler_params=params(16),
            cost_estimate=cost(1e8, 1e6),
        )(where, gathered, all_grads, own_id)

    with jax.named_scope("grad_spectral"):
        width = block_n * MODES

        def lanes_spec(height):
            return pl.BlockSpec((height, width), lambda h, n, core: (0, n))

        grad_spectral = pl.pallas_call(
            outer_kernel,
            grid_spec=pltpu.PrefetchScalarGridSpec(
                num_scalar_prefetch=1,
                grid=(2, steps),
                in_specs=[lanes_spec(chan)] * 2 + [lanes_spec(2 * chan)] * 2,
                out_specs=pl.BlockSpec(
                    (block_n, MODES, chan, 2 * chan), lambda h, n, core: (h * steps + n, 0, 0, 0)
                ),
            ),
            out_shape=jax.ShapeDtypeStruct((2 * own, MODES, chan, 2 * chan), BF16),
            compiler_params=params(32),
            cost_estimate=cost(1e7, 1.8e7),
        )(core, coef_near, coef_far, grad_modes, grad_far)

    with jax.named_scope("encoder_back"):
        (enc_grads,) = back(
            1.0, QUADRATURE, False, features_t, enc_w1, encoder_second,
            enc_g, enc_slope, own_grads, arrived_back,
        )
    with jax.named_scope("weight_sums"):
        both = jnp.concatenate([enc_grads, dec_grads], axis=1).astype(BF16)
        spread = jnp.broadcast_to(both[None], (devices,) + both.shape)
        total = jnp.sum(
            lax.all_to_all(spread, ("slab", "sub"), 0, 0, tiled=True).astype(F32), axis=0
        )
        small = total[chan:]
        small = small + lax.ppermute(small, "chan", swap)
    enc_second = total[:chan, :hidden].T
    dec_second = total[:chan, hidden:].T
    return (
        decoded.T,
        small[0:3, :hidden],
        small[3, :hidden],
        enc_second,
        small[0:3, hidden:],
        small[3, hidden:],
        dec_second,
        grad_spectral,
    )


def solution(mesh):
    placed = (
        P(None, ("groups", "slab", "sub")),
        P(("groups", "slab", "sub"), "chan"),
        P(("groups", "slab", "sub")),
        P(("groups", "slab"), None, None, None),
        P(("groups", "slab"), None, None, None),
        P(("groups", "slab"), None, None),
        P("chan", ("groups", "slab", "sub"), None, None),
        P(),
        P(),
        P(None, "chan"),
        P(),
        P(),
        P(None, "chan"),
        P(("slab", "sub"), None, None, None),
        P(("groups", "slab", "sub"), "chan"),
    )
    return jax.shard_map(
        body,
        mesh=mesh,
        in_specs=placed,
        out_specs=(
            P(("groups", "slab", "sub"), "chan"),
            P("groups", None),
            P("groups"),
            P("groups", "chan"),
            P("groups", None),
            P("groups"),
            P("groups", "chan"),
            P(("groups", "slab", "sub"), None, "chan", None),
        ),
        check_vma=False,
    )
```

profile of v0, /device:TPU:0, one launch (start us, length us, event | category | flops | bytes accessed | tf_op | source)
XLA Modules:
  0.0 181.5 jit_solution(5367629190266022029)
XLA Ops:
  0.7 0.7 copy-done
  1.6 3.4 %copy-done.6 = bf16[32,8,128,128]{3,2,1,0:T(8,128)(2,1)S(1)} copy-done((bf16[32,8,128,128]{3,2,1,0:T(8,128)(2,1)S(1)}, bf16[32,8,128,128]{3,2,1,0:T(8,128)(2,1)}, u32[]{:S(2)}) %copy-start.6) | copy-done | bytes 8388632
  5.0 1.6 copy-done.11
  6.6 1.0 copy-done.14
  7.6 1.0 copy-done.15
  8.6 0.9 copy-done.16
  9.6 12.3 %dense_transform.1 = (bf16[256,1024]{1,0:T(8,128)(2,1)}, bf16[4,32,128]{2,1,0:T(8,128)(2,1)}) custom-call(s32[1]{0:T(128)} %bitcast.4.me, s32[3,16]{1,0:T(4,128)S(1)} %pad_add_fusion.held, bf16[32,8,128,128]{3,2,1,0:T(8,128)(2,1)S(1)} %copy-done.6, bf16[512,256]{1,0:T(8,128)(2,1)S(1)} %copy-done.16, bf16[256,1024]{1,0:T(8,128)(2,1)S(1)} %copy-done.15, ...), custom_call_target="tpu_custom_call" | custom-call | flops 8000000000 | bytes 10000000 | tf_op jit(solution)/shard_map/dense_transform/pallas_call | solution.py:613
  21.9 5.1 %all-to-all-start.2 = ((bf16[4,32,128]{2,1,0:T(8,128)(2,1)}), bf16[4,32,128]{2,1,0:T(8,128)(2,1)S(1)}, u32[]{:S(2)}, u32[]{:S(2)}) async-start(bf16[4,32,128]{2,1,0:T(8,128)(2,1)} %get-tuple-element.32), calls=%async_computation.2 | async-start | bytes 65536 | tf_op jit(solution)/shard_map/held_exchange/all_to_all | solution.py:653
  27.0 0.7 fusion.5
  27.9 0.7 constant_dynamic-slice_fusion.5
  29.5 6.3 %encoder_points.1 = (bf16[8192,32]{1,0:T(8,128)(2,1)S(1)}, bf16[8192,128]{1,0:T(8,128)(2,1)S(1)}, bf16[16,48,128]{2,1,0:T(8,128)(2,1)S(1)}) custom-call(s32[16]{0:T(128)S(1)} %reshape.547.blk, f32[3,16]{1,0:T(4,128)S(1)} %fusion.cell, f32[16]{0:T(128)S(1)} %compare_convert_fusion.live, s32[8]{0:T(128)S(1)} %copy-done.10, f32[3,1024]{1,0:T(4,128)S(1)} %copy-done.9, ...), custom_call_target="tpu_custom_call" | custom-call | flops 2000000000 | bytes 8000000 | tf_op jit(solution)/shard_map/encoder_points/pallas_call | solution.py:593
  35.9 1.3 copy-done.23
  37.2 1.4 copy-done.25
  38.6 15.2 %all_to_all.35 = bf16[16,48,128]{2,1,0:T(8,128)(2,1)S(1)} all-to-all(bf16[16,48,128]{2,1,0:T(8,128)(2,1)S(1)} %get-tuple-element.31), channel_id=1, replica_groups=mesh['groups'=1,'slab'=4,'sub'=4,'chan'=2] {'slab','sub'}, dimensions={0} | all-to-all | bytes 393216 | tf_op jit(solution)/shard_map/partials_all/all_to_all | solution.py:608
  53.8 2.6 %all-to-all-start = ((bf16[32,8,1024]{2,1,0:T(8,128)(2,1)}), bf16[32,8,1024]{2,1,0:T(8,128)(2,1)S(1)}, u32[]{:S(2)}, u32[]{:S(2)}) async-start(bf16[32,8,1024]{2,1,0:T(8,128)(2,1)} %bitcast.5), calls=%async_computation | async-start | bytes 1048576 | tf_op jit(solution)/shard_map/dense_exchange/all_to_all | solution.py:648
  56.6 0.6 dynamic_slice.33
  57.2 0.6 broadcast_multiply_fusion
  58.1 0.7 fusion.1
  58.9 2.1 %all-gather = bf16[32,48,128]{2,1,0:T(8,128)(2,1)S(1)} all-gather(bf16[16,48,128]{2,1,0:T(8,128)(2,1)S(1)} %all_to_all.35), channel_id=2, replica_groups=mesh['groups'=1,'slab'=4,'sub'=4,'chan'=2] {'chan'}, dimensions={0}, use_global_device_ids=true | all-gather | bytes 589824 | tf_op jit(solution)/shard_map/partials_all/all_gather | solution.py:609
  61.0 1.0 copy-done.13
  62.0 5.6 %cell_basis.1 = (bf16[1024,2048]{1,0:T(8,128)(2,1)S(1)}, f32[1024,64]{1,0:T(8,128)S(1)}, f32[32,128]{1,0:T(8,128)S(1)}) custom-call(s32[6]{0:T(128)S(1)} %pad_add_fusion.1.where, bf16[2,16,48,128]{3,2,1,0:T(8,128)(2,1)S(1)} %bitcast.25, bf16[1024,256]{1,0:T(8,128)(2,1)S(1)} %copy-done.13, bf16[1024,256]{1,0:T(8,128)(2,1)S(1)} %copy-done.12, ...), custom_call_target="tpu_custom_call" | custom-call | flops 5000000000 | bytes 8000000 | tf_op jit(solution)/shard_map/cell_basis/pallas_call | solution.py:674
  67.6 2.0 %copy-done.2 = bf16[1024,2048]{1,0:T(8,128)(2,1)} copy-done((bf16[1024,2048]{1,0:T(8,128)(2,1)}, bf16[1024,2048]{1,0:T(8,128)(2,1)S(1)}, u32[]{:S(2)}) %copy-start.2) | copy-done | bytes 4194328
  69.6 2.3 %all-to-all-done = bf16[32,8,1024]{2,1,0:T(8,128)(2,1)S(1)} async-done(((bf16[32,8,1024]{2,1,0:T(8,128)(2,1)}), bf16[32,8,1024]{2,1,0:T(8,128)(2,1)S(1)}, u32[]{:S(2)}, u32[]{:S(2)}) %all-to-all-start) | async-done | bytes 524320 | tf_op jit(solution)/shard_map/dense_exchange/all_to_all | solution.py:648
  72.0 2.2 %copy-done.3 = bf16[1024,2048]{1,0:T(8,128)(2,1)S(1)} copy-done((bf16[1024,2048]{1,0:T(8,128)(2,1)S(1)}, bf16[1024,2048]{1,0:T(8,128)(2,1)}, u32[]{:S(2)}) %copy-start.3) | copy-done | bytes 4194328
  74.1 12.1 %mix.1 = (bf16[32,32,128]{2,1,0:T(8,128)(2,1)}, f32[64,1024]{1,0:T(8,128)S(1)}) custom-call(s32[1]{0:T(128)} %bitcast.3.chan_index, bf16[16,2,8,1024]{3,2,1,0:T(8,128)(2,1)S(1)} %bitcast.24, bf16[64,128]{1,0:T(8,128)(2,1)S(1)} %copy-done.5, f32[1024,64]{1,0:T(8,128)S(1)} %get-tuple-element.33.dcoef_ref, bf16[64,32,64,64]{3,2,1,0:T(8,128)(2,1)} %w_ref.3, ...), custom_call_target="tpu_custom_call" | custom-call | flops 4000000000 | bytes 24000000 | tf_op jit(solution)/shard_map/mix/pallas_call | solution.py:711
  86.3 3.5 %all-to-all-start.3 = ((bf16[32,32,128]{2,1,0:T(8,128)(2,1)}), bf16[32,32,128]{2,1,0:T(8,128)(2,1)S(1)}, u32[]{:S(2)}, u32[]{:S(2)}) async-start(bf16[32,32,128]{2,1,0:T(8,128)(2,1)} %get-tuple-element.35), calls=%async_computation.3 | async-start | bytes 524288 | tf_op jit(solution)/shard_map/preact_exchange/all_to_all | solution.py:739
  89.9 6.4 %decoder_points.1 = (bf16[8192,32]{1,0:T(8,128)(2,1)S(1)}, bf16[8192,128]{1,0:T(8,128)(2,1)S(1)}, f32[32,128]{1,0:T(8,128)S(1)}, bf16[8192,128]{1,0:T(8,128)(2,1)S(1)}) custom-call(s32[16]{0:T(128)S(1)} %reshape.547.blk, f32[3,16]{1,0:T(4,128)S(1)} %fusion.cell, f32[16]{0:T(128)S(1)} %compare_convert_fusion.live, s32[8]{0:T(128)S(1)} %copy-done.10, ...), custom_call_target="tpu_custom_call" | custom-call | flops 2000000000 | bytes 8000000 | tf_op jit(solution)/shard_map/decoder_points/pallas_call | solution.py:593
  96.3 1.4 copy-done.17
  97.7 1.4 copy-done.19
  99.0 1.3 copy-done.21
  100.6 16.2 %all_to_all.36.recv_ref = bf16[32,32,128]{2,1,0:T(8,128)(2,1)S(1)} all-to-all(bf16[32,32,128]{2,1,0:T(8,128)(2,1)S(1)} %get-tuple-element.43), channel_id=1, replica_groups=mesh['groups'=1,'slab'=4,'sub'=4,'chan'=2] {'slab','sub','chan'}, dimensions={0} | all-to-all | bytes 524288 | tf_op jit(solution)/shard_map/cell_grads_all/all_to_all | solution.py:756
  116.8 2.2 %copy-done.4 = bf16[1024,2048]{1,0:T(8,128)(2,1)S(1)} copy-done((bf16[1024,2048]{1,0:T(8,128)(2,1)S(1)}, bf16[1024,2048]{1,0:T(8,128)(2,1)}, u32[]{:S(2)}) %copy-start.4) | copy-done | bytes 4194328
  119.0 14.3 %mix_back.1 = (bf16[32,32,128]{2,1,0:T(8,128)(2,1)}, f32[64,1024]{1,0:T(8,128)S(1)}) custom-call(s32[1]{0:T(128)} %bitcast.3.chan_index, bf16[32,32,128]{2,1,0:T(8,128)(2,1)S(1)} %all_to_all.36.recv_ref, bf16[64,32,64,64]{3,2,1,0:T(8,128)(2,1)} %w_ref.3, bf16[1024,2048]{1,0:T(8,128)(2,1)S(1)} %copy-done.4, f32[1024,1]{1,0:T(8,128)S(1)} %copy.57.scale_ref.column_ref, ...), custom_call_target="tpu_custom_call" | custom-call | flops 4000000000 | bytes 24000000 | tf_op jit(solution)/shard_map/mix_back/pallas_call | solution.py:711
  133.3 2.6 %all-to-all-start.5 = ((bf16[32,32,128]{2,1,0:T(8,128)(2,1)}), bf16[32,32,128]{2,1,0:T(8,128)(2,1)S(1)}, u32[]{:S(2)}, u32[]{:S(2)}) async-start(bf16[32,32,128]{2,1,0:T(8,128)(2,1)} %get-tuple-element.44), calls=%async_computation.5 | async-start | bytes 524288 | tf_op jit(solution)/shard_map/latent_grad_exchange/all_to_all | solution.py:794
  135.9 1.6 copy-done.18
  137.5 1.6 copy-done.20
  139.1 1.6 copy-done.22
  140.7 5.0 %decoder_back.1 = (f32[40,64]{1,0:T(8,128)S(1)}, bf16[32,1024]{1,0:T(8,128)(2,1)}) custom-call(s32[16]{0:T(128)S(1)} %reshape.547.blk, f32[3,16]{1,0:T(4,128)S(1)} %fusion.cell, f32[16]{0:T(128)S(1)} %compare_convert_fusion.live, s32[8]{0:T(128)S(1)} %copy-done.10, f32[3,1024]{1,0:T(4,128)S(1)} %copy-done.9, bf16[32,1024]{1,0:T(8,128)(2,1)S(1)} %bitcast.31, ...), custom_call_target="tpu_custom_call" | custom-call | flops 2000000000 | bytes 8000000 | tf_op jit(solution)/shard_map/decoder_back/pallas_call | solution.py:765
  145.7 0.8 own_cells.1.rest_6_
  146.5 1.6 copy-done.24
  148.1 1.6 copy-done.26
  149.7 4.3 %encoder_back.1 = f32[40,64]{1,0:T(8,128)S(1)} custom-call(s32[16]{0:T(128)S(1)} %reshape.547.blk, f32[3,16]{1,0:T(4,128)S(1)} %fusion.cell, f32[16]{0:T(128)S(1)} %compare_convert_fusion.live, s32[8]{0:T(128)S(1)} %copy-done.10, f32[3,1024]{1,0:T(4,128)S(1)} %copy-done.9, bf16[32,1024]{1,0:T(8,128)(2,1)S(1)} %bitcast.33, ...), custom_call_target="tpu_custom_call" | custom-call | flops 2000000000 | bytes 8000000 | tf_op jit(solution)/shard_map/encoder_back/pallas_call | solution.py:765
  154.0 0.7 broadcast_in_dim.66
  154.7 6.9 %all-to-all-start.6 = ((bf16[16,40,128]{2,1,0:T(8,128)(2,1)}), bf16[16,40,128]{2,1,0:T(8,128)(2,1)S(1)}, u32[]{:S(2)}, u32[]{:S(2)}) async-start(bf16[16,40,128]{2,1,0:T(8,128)(2,1)} %broadcast_in_dim.66), calls=%async_computation.6 | async-start | bytes 327680 | tf_op jit(solution)/shard_map/weight_sums/all_to_all | solution.py:837
  162.3 1.1 collective-permute-done.1.c_far
  163.4 15.6 %grad_spectral.1 = bf16[64,32,32,64]{3,2,1,0:T(8,128)(2,1)} custom-call(s32[1]{0:T(128)} %bitcast.3.chan_index, f32[32,1024]{1,0:T(8,128)S(1)} %get-tuple-element.52.c_own, f32[32,1024]{1,0:T(8,128)S(1)} %collective-permute-done.1.c_far, f32[64,1024]{1,0:T(8,128)S(1)} %get-tuple-element.47.g_own, f32[64,1024]{1,0:T(8,128)S(1)} %collective-permute-done.2.g_far), custom_call_target="tpu_custom_call" | custom-call | flops 10000000 | bytes 18000000 | tf_op jit(solution)/shard_map/grad_spectral/pallas_call | solution.py:813
  179.3 0.7 slice_bitcast_fusion
  180.8 0.7 fusion.15
  (102 shorter events, 4.1 us)
Async XLA Ops:
  0.6 0.7 copy-start
  1.6 3.4 %copy-start.6 = (bf16[32,8,128,128]{3,2,1,0:T(8,128)(2,1)S(1)}, bf16[32,8,128,128]{3,2,1,0:T(8,128)(2,1)}, u32[]{:S(2)}) copy-start(bf16[32,8,128,128]{3,2,1,0:T(8,128)(2,1)} %x_ref.4) | copy-start | bytes 25165828
  5.0 1.6 copy-start.11
  6.6 1.0 copy-start.14
  7.6 1.0 copy-start.15
  8.6 0.9 copy-start.16
  9.6 19.1 %copy-start.30 = (f32[3,64]{1,0:T(4,128)S(1)}, f32[3,64]{1,0:T(4,128)}, u32[]{:S(2)}) copy-start(f32[3,64]{1,0:T(4,128)} %param.32) | copy-start | bytes 2308
  9.6 19.6 %copy-start.27 = (f32[64,32]{0,1:T(8,128)S(1)}, f32[64,32]{0,1:T(8,128)}, u32[]{:S(2)}) copy-start(f32[64,32]{0,1:T(8,128)} %param.34) | copy-start | bytes 24580
  9.6 19.7 %copy-start.32 = (f32[64]{0:T(128)S(1)}, f32[64]{0:T(128)}, u32[]{:S(2)}) copy-start(f32[64]{0:T(128)} %param.33) | copy-start | bytes 772
  9.6 19.9 %copy-start.8 = (bf16[1024,32]{0,1:T(8,128)(2,1)S(1)}, bf16[1024,32]{0,1:T(8,128)(2,1)}, u32[]{:S(2)}) copy-start(bf16[1024,32]{0,1:T(8,128)(2,1)} %param.26) | copy-start | bytes 196612
  9.6 19.9 %copy-start.9 = (f32[3,1024]{1,0:T(4,128)S(1)}, f32[3,1024]{1,0:T(4,128)}, u32[]{:S(2)}) copy-start(f32[3,1024]{1,0:T(4,128)} %rest_0_.3) | copy-start | bytes 36868
  9.6 19.9 %copy-start.10 = (s32[8]{0:T(128)S(1)}, s32[8]{0:T(128)}, u32[]{:S(2)}) copy-start(s32[8]{0:T(128)} %count.7) | copy-start | bytes 100
  21.9 16.7 %all-to-all-start.2 = ((bf16[4,32,128]{2,1,0:T(8,128)(2,1)}), bf16[4,32,128]{2,1,0:T(8,128)(2,1)S(1)}, u32[]{:S(2)}, u32[]{:S(2)}) async-start(bf16[4,32,128]{2,1,0:T(8,128)(2,1)} %get-tuple-element.32), calls=%async_computation.2 | async-start | bytes 65536 | tf_op jit(solution)/shard_map/held_exchange/all_to_all | solution.py:653
  29.5 27.0 %copy-start.28 = (f32[64,32]{0,1:T(8,128)S(1)}, f32[64,32]{0,1:T(8,128)}, u32[]{:S(2)}) copy-start(f32[64,32]{0,1:T(8,128)} %param.37) | copy-start | bytes 24580
  29.5 27.1 %copy-start.34 = (f32[32]{0:T(128)S(1)}, f32[32]{0:T(128)}, u32[]{:S(2)}) copy-start(f32[32]{0:T(128)} %constant.195.clone) | copy-start | bytes 388
  29.5 27.7 %copy-start.29 = (f32[1024]{0:T(1024)S(1)}, f32[1024]{0:T(1024)}, u32[]{:S(2)}) copy-start(f32[1024]{0:T(1024)} %constant.194.clone) | copy-start | bytes 12292
  35.8 1.3 copy-start.23
  37.2 1.4 copy-start.25
  38.6 22.4 %copy-start.12 = (bf16[1024,256]{1,0:T(8,128)(2,1)S(1)}, bf16[1024,256]{1,0:T(8,128)(2,1)}, u32[]{:S(2)}) copy-start(bf16[1024,256]{1,0:T(8,128)(2,1)} %constant.197.clone.ix_ref) | copy-start | bytes 1572868
  53.8 18.2 %all-to-all-start = ((bf16[32,8,1024]{2,1,0:T(8,128)(2,1)}), bf16[32,8,1024]{2,1,0:T(8,128)(2,1)S(1)}, u32[]{:S(2)}, u32[]{:S(2)}) async-start(bf16[32,8,1024]{2,1,0:T(8,128)(2,1)} %bitcast.5), calls=%async_computation | async-start | bytes 1048576 | tf_op jit(solution)/shard_map/dense_exchange/all_to_all | solution.py:648
  61.0 1.0 copy-start.13
  62.0 9.9 %copy-start.5 = (bf16[64,128]{1,0:T(8,128)(2,1)S(1)}, bf16[64,128]{1,0:T(8,128)(2,1)}, u32[]{:S(2)}) copy-start(bf16[64,128]{1,0:T(8,128)(2,1)} %constant.198.clone.fi_ref) | copy-start | bytes 49156
  67.6 2.0 %copy-start.2 = (bf16[1024,2048]{1,0:T(8,128)(2,1)}, bf16[1024,2048]{1,0:T(8,128)(2,1)S(1)}, u32[]{:S(2)}) copy-start(bf16[1024,2048]{1,0:T(8,128)(2,1)S(1)} %get-tuple-element.34.bt_ref) | copy-start | bytes 12582916
  72.0 2.2 %copy-start.3 = (bf16[1024,2048]{1,0:T(8,128)(2,1)S(1)}, bf16[1024,2048]{1,0:T(8,128)(2,1)}, u32[]{:S(2)}) copy-start(bf16[1024,2048]{1,0:T(8,128)(2,1)} %copy-done.2) | copy-start | bytes 12582916
  74.1 15.6 %copy-start.31 = (f32[3,64]{1,0:T(4,128)S(1)}, f32[3,64]{1,0:T(4,128)}, u32[]{:S(2)}) copy-start(f32[3,64]{1,0:T(4,128)} %param.35) | copy-start | bytes 2308
  74.1 15.6 %copy-start.33 = (f32[64]{0:T(128)S(1)}, f32[64]{0:T(128)}, u32[]{:S(2)}) copy-start(f32[64]{0:T(128)} %param.36) | copy-start | bytes 772
  74.1 15.7 %copy-start.7 = (bf16[1024,32]{0,1:T(8,128)(2,1)S(1)}, bf16[1024,32]{0,1:T(8,128)(2,1)}, u32[]{:S(2)}) copy-start(bf16[1024,32]{0,1:T(8,128)(2,1)} %param.39) | copy-start | bytes 196612
  86.3 14.1 %all-to-all-start.3 = ((bf16[32,32,128]{2,1,0:T(8,128)(2,1)}), bf16[32,32,128]{2,1,0:T(8,128)(2,1)S(1)}, u32[]{:S(2)}, u32[]{:S(2)}) async-start(bf16[32,32,128]{2,1,0:T(8,128)(2,1)} %get-tuple-element.35), calls=%async_computation.3 | async-start | bytes 524288 | tf_op jit(solution)/shard_map/preact_exchange/all_to_all | solution.py:739
  96.3 1.4 copy-start.17
  97.7 1.4 copy-start.19
  99.0 1.3 copy-start.21
  116.8 2.2 %copy-start.4 = (bf16[1024,2048]{1,0:T(8,128)(2,1)S(1)}, bf16[1024,2048]{1,0:T(8,128)(2,1)}, u32[]{:S(2)}) copy-start(bf16[1024,2048]{1,0:T(8,128)(2,1)} %copy-done.2) | copy-start | bytes 12582916
  133.3 13.2 %all-to-all-start.5 = ((bf16[32,32,128]{2,1,0:T(8,128)(2,1)}), bf16[32,32,128]{2,1,0:T(8,128)(2,1)S(1)}, u32[]{:S(2)}, u32[]{:S(2)}) async-start(bf16[32,32,128]{2,1,0:T(8,128)(2,1)} %get-tuple-element.44), calls=%async_computation.5 | async-start | bytes 524288 | tf_op jit(solution)/shard_map/latent_grad_exchange/all_to_all | solution.py:794
  135.9 1.6 copy-start.18
  137.5 1.6 copy-start.20
  139.1 1.6 copy-start.22
  146.5 1.6 copy-start.24
  148.1 1.6 copy-start.26
  154.7 24.2 %all-to-all-start.6 = ((bf16[16,40,128]{2,1,0:T(8,128)(2,1)}), bf16[16,40,128]{2,1,0:T(8,128)(2,1)S(1)}, u32[]{:S(2)}, u32[]{:S(2)}) async-start(bf16[16,40,128]{2,1,0:T(8,128)(2,1)} %broadcast_in_dim.66), calls=%async_computation.6 | async-start | bytes 327680 | tf_op jit(solution)/shard_map/weight_sums/all_to_all | solution.py:837
  161.6 1.8 collective-permute-start.2
  161.7 1.7 collective-permute-start.1
  163.4 18.1 %copy-start.1 = (s32[1,4,4,4]{3,2,1,0:T(4,128)S(1)}, s32[1,4,4,4]{3,2,1,0:T(4,128)}, u32[]{:S(2)}) copy-start(s32[1,4,4,4]{3,2,1,0:T(4,128)} %param.29) | copy-start | bytes 772
  179.0 1.2 collective-permute-start
where the time goes:
time: 183 us; the launch traced here: 181 us
  Pallas kernels  82.8 us (45%)
  local copies, waits for them, and re-layouts  37.8 us (21%)
  blocking collectives  33.5 us (18%)
  starting transfers between devices  21.5 us (12%)
  waiting for transfers between devices  3.75 us (2%)
    unnamed x72, local copies, waits for them, and re-layouts  31.1 us
    pallas_call x2, Pallas kernels, mode_call(): pl.pallas_call(kernel, grid_spec=pltpu.PrefetchScalarGridSpec(num_scalar_...  26.4 us
    all_to_all x1, blocking collectives, body(): all_grads = lax.all_to_all(cell_grads, every, 0, 0, tiled=True)  16.2 us
    pallas_call x1, Pallas kernels, body(): pl.pallas_call(outer_kernel, grid_spec=pltpu.PrefetchScalarGridSpec(num_s...  15.6 us
    all_to_all x1, blocking collectives, body(): near = lax.all_to_all(message, ('slab', 'sub'), 0, 0, tiled=True)  15.2 us
    pallas_call x2, Pallas kernels, net(): pl.pallas_call(functools.partial(net_kernel, sign, weight, keep, slots),...  12.7 us
    pallas_call x1, Pallas kernels, body(): pl.pallas_call(functools.partial(dense_kernel, planes), grid=(planes,), o...  12.3 us
    pallas_call x2, Pallas kernels, back(): pl.pallas_call(functools.partial(back_kernel, sign, weight, decode, slots...  9.29 us
  transfers between devices with their start and end apart: 8, of which 3 were waited for; matrix products, arithmetic and copies ran while one was open for 3% of the time, Pallas kernels for 22%

commit v1 on v0

v1 whole, which is shorter than its diff:
```python
import functools

import jax
import jax.numpy as jnp
import numpy as np
from jax import lax
from jax.experimental import pallas as pl
from jax.experimental.pallas import tpu as pltpu
from jax.sharding import PartitionSpec as P

MODES = 32
BLOCK = 128
BRICK = 8
CAP = 4
RADIUS = 4.0
QUADRATURE = 0.0625

F32 = jnp.float32
BF16 = jnp.bfloat16
MIB = 1 << 20

NN = (((1,), (0,)), ((), ()))
NT = (((1,), (1,)), ((), ()))
TN = (((0,), (0,)), ((), ()))


def dot(a, b, dims=NN):
    return lax.dot_general(a, b, dims, preferred_element_type=F32)


def raw_basis(length):
    half = MODES // 2
    n = np.arange(length)[:, None]
    m = np.arange(half)[None, :]
    values = np.concatenate(
        [np.cos(2 * np.pi * m * n / length), np.sin(2 * np.pi * (m + 1) * n / length)], axis=1
    )
    norm = np.full(MODES, np.sqrt(2.0 / length))
    norm[0] = np.sqrt(1.0 / length)
    return values, norm


def halves(values):
    high = np.asarray(values, np.float32).astype(jnp.bfloat16)
    low = (np.asarray(values, np.float64) - high.astype(np.float64)).astype(jnp.bfloat16)
    return high, low


def split(value):
    high = value.astype(BF16).astype(F32)
    return high, value - high


def over(x, d):
    return x >> (d.bit_length() - 1) if d & (d - 1) == 0 else lax.div(x, d)


def modulo(x, d):
    return x & (d - 1) if d & (d - 1) == 0 else lax.rem(x, d)


def gelu_pair(x):
    a = 0.7978845608028654
    b = a * 0.044715
    x2 = x * x
    t = jnp.tanh(x * (a + b * x2))
    half = 0.5 + 0.5 * t
    slope = half + (0.5 * x) * (1.0 - t * t) * (a + (3.0 * b) * x2)
    return x * half, slope


VMEM_LIMIT = 62 * MIB


class Late:
    def __init__(self, source, target, sems, pieces, axis, held, ahead):
        self.source, self.target, self.sems, self.ahead = source, target, sems, ahead
        self.pieces, self.axis, self.ref = pieces, axis, held

    def copy(self, i):
        size = self.ref.shape[self.axis] // self.pieces
        if isinstance(i, int):
            piece = pl.ds(i * size, size)
        else:
            piece = pl.ds(pl.multiple_of(i * size, size), size)
        at = (slice(None),) * self.axis + (piece,)
        return pltpu.make_async_copy(self.source.at[at], self.target.at[at], self.sems.at[i])

    def start(self, i):
        self.copy(i).start()

    def wait(self, i):
        self.copy(i).wait()


def call(kernel, ins, outs, scratch=(), flops=1e9, nbytes=8e6):
    buffers, sems = [], []
    modes_in, modes_out = [m for _, m in ins], [m for _, m in outs]
    for array, mode in [*ins, *outs]:
        if mode == "raw":
            continue
        space = pltpu.SMEM if mode == "scalar" else pltpu.VMEM
        buffers.append(space(array.shape, array.dtype))
        sems.append(pltpu.SemaphoreType.DMA((mode[0] if isinstance(mode, tuple) else 1,)))

    def wrapped(*refs):
        arrays = refs[: len(ins) + len(outs)]
        rest = refs[len(ins) + len(outs) :]
        held, signals = rest[: len(buffers)], rest[len(buffers) : 2 * len(buffers)]
        more = rest[2 * len(buffers) :]
        objects, early, late, place = [], [], [], 0
        for i, (array, mode) in enumerate(zip(arrays, modes_in + modes_out)):
            if mode == "raw":
                objects.append(array)
                continue
            buffer, sem = held[place], signals[place]
            place += 1
            pieces, axis = mode if isinstance(mode, tuple) else (1, 0)
            source, target = (array, buffer) if i < len(ins) else (buffer, array)
            one = Late(source, target, sem, pieces, axis, buffer, i < len(ins))
            if isinstance(mode, tuple):
                objects.append(one)
                late.append((i, one))
            else:
                objects.append(buffer)
                early.append((i, pltpu.make_async_copy(source, target, sem.at[0])))
        for i, one in early:
            if i < len(ins):
                one.start()
        for i, one in late:
            if i < len(ins):
                for j in range(one.pieces):
                    one.start(j)
        for i, one in early:
            if i < len(ins):
                one.wait()
        kernel(*objects, *more)
        for i, one in early:
            if i >= len(ins):
                one.start()
        for i, one in early:
            if i >= len(ins):
                one.wait()
        for i, one in late:
            if i >= len(ins):
                for j in range(one.pieces):
                    one.wait(j)

    hbm = pl.BlockSpec(memory_space=pl.ANY)
    return pl.pallas_call(
        wrapped,
        out_shape=[jax.ShapeDtypeStruct(o.shape, o.dtype) for o, _ in outs],
        in_specs=[hbm] * len(ins),
        out_specs=[hbm] * len(outs),
        scratch_shapes=[*buffers, *sems, *scratch],
        compiler_params=pltpu.CompilerParams(vmem_limit_bytes=VMEM_LIMIT),
        cost_estimate=pl.CostEstimate(
            flops=int(flops), bytes_accessed=int(nbytes), transcendentals=0
        ),
    )(*[a for a, _ in ins])


class Slots:
    def __init__(self, refs, subs, planes, count_j, per_row):
        self.block_ref, self.brick_ref, self.count_ref, self.valid_ref = refs
        self.subs, self.planes = subs, planes
        self.count_j, self.per_row = count_j, per_row
        self.slots = subs * CAP
        self.slab = lax.axis_index("slab")
        self.me = lax.axis_index("sub")
        self.core = lax.axis_index("chan")

    def block(self, s):
        return self.block_ref[0, self.me, over(s, CAP), modulo(s, CAP)]

    def place(self, brick):
        row = modulo(over(brick, self.per_row), self.count_j)
        column = modulo(brick, self.per_row) * BRICK
        return over(brick, self.count_j * self.per_row), row, column

    def own(self, s):
        layer, row, column = self.place(self.brick_ref[0, self.me, over(s, CAP), modulo(s, CAP)])
        first = (self.slab * self.subs + over(s, CAP)) * self.planes
        return first + layer, row, column

    def held(self, t):
        return self.place(self.brick_ref[0, over(t, CAP), self.me, modulo(t, CAP)])

    def live(self, s):
        count = self.count_ref[0, self.me, over(s, CAP)]
        return jnp.where(modulo(s, CAP) < count, 1.0, 0.0)

    def valid(self, b):
        return self.valid_ref[b]

    def lines(self, which):
        cells = self.slots * BRICK
        lane = lax.broadcasted_iota(jnp.int32, (1, cells), 1)
        rows = [jnp.zeros((1, cells), jnp.int32)] * 3
        for s in range(self.slots):
            here = over(lane, BRICK) == s
            values = which(jnp.int32(s))
            rows = [jnp.where(here, v, r) for v, r in zip(values, rows)]
        rows[2] = rows[2] + modulo(lane, BRICK)
        return [r.astype(F32) for r in rows]


def cell_number(lines):
    return lines[0] * 16384.0 + lines[1] * 128.0 + lines[2]


def same_cells(column_lines, lines):
    number = cell_number(column_lines)
    tall = jnp.transpose(jnp.broadcast_to(number, (number.shape[1], number.shape[1])))
    return jnp.where(tall[:, 0:1] == cell_number(lines), 1.0, 0.0).astype(BF16)


def columns(first, bias, w1):
    hidden = first.shape[1]
    rows = jnp.concatenate(
        [first[...] * (1.0 / RADIUS), bias[...], jnp.zeros((124, hidden), F32)], axis=0
    )
    turned = jnp.transpose(rows)
    for d in range(4):
        w1[d] = jnp.broadcast_to(turned[:, d : d + 1], (hidden, BLOCK))


def second_layer(ref):
    return jnp.concatenate([ref[...], ref[...]], axis=1)


def slot_points(slots, s, x_ref):
    at = pl.multiple_of(slots.block(s) * BLOCK, BLOCK)
    xs = x_ref[:, pl.ds(at, BLOCK)]
    place = slots.own(s)
    return at, [(place[d].astype(F32) + 0.5) - xs[d : d + 1, :] for d in range(3)]


def slot_mask(slots, s, weight):
    lanes = lax.broadcasted_iota(jnp.int32, (1, BLOCK), 1)
    return jnp.where(lanes < slots.valid(slots.block(s)), weight, 0.0) * slots.live(s)


def slot_source(slots, s, at, f_ref, weight):
    return (f_ref[:, pl.ds(at, BLOCK)].astype(F32) * slot_mask(slots, s, weight)).astype(BF16)


def first_base(sign, e, w1):
    return w1[3] + sign * (w1[0] * e[0] + w1[1] * e[1] + w1[2] * e[2])


def spread_groups(me, values, outs):
    groups = len(outs)
    cells = values.shape[1]
    width = cells // groups
    lane = over(lax.broadcasted_iota(jnp.int32, (1, cells), 1), width)
    for k in range(groups):
        moved = pltpu.roll(values, (groups - k) % groups * width, 1) if k else values
        outs[k][...] = jnp.where(lane == me, moved, 0.0).astype(BF16)


def loop(slots, step, first, *arrays):
    each = slots // arrays[0].pieces

    def piece(i, carry):
        for array in arrays:
            if array.ahead:
                array.wait(i)
        for j in range(each):
            carry = step(i * each + j, carry)
        for array in arrays:
            if not array.ahead:
                array.start(i)
        return carry

    return lax.fori_loop(0, arrays[0].pieces, piece, first)


def net_kernel(sign, weight, keep, make, s0, s1, s2, s3, x_ref, f_ref, first, bias, second, *rest):
    slots = make((s0, s1, s2, s3))
    if keep:
        g, slope, hid, part_ref, w1, group = rest
    else:
        g, outs, (w1, group) = rest[0], rest[1:-2], rest[-2:]
    chan, hidden = second.shape
    wide = BRICK * hidden
    cells = slots.slots * BRICK
    columns(first, bias, w1)
    w2 = jnp.concatenate([second_layer(second)] * (BRICK // 2), axis=1)
    of_row = over(lax.broadcasted_iota(jnp.int32, (wide, 128), 0), hidden)
    at_lane = lax.broadcasted_iota(jnp.int32, (wide, 128), 1)
    group[...] = jnp.where(of_row == at_lane, 1.0, 0.0).astype(BF16)

    def step(s, part):
        at, e = slot_points(slots, s, x_ref)
        f = slot_source(slots, s, at, f_ref, weight)
        base = first_base(sign, e, w1)
        row = pl.multiple_of(s * wide, wide)
        values = []
        for q in range(BRICK):
            value, gradient = gelu_pair(base + (sign * q) * w1[2])
            values.append(value.astype(BF16))
            if keep:
                slope.ref[pl.ds(row + q * hidden, hidden), :] = gradient.astype(BF16)
        all_q = jnp.concatenate(values, axis=0)
        total = dot(f, all_q, NT)
        g.ref[pl.ds(pl.multiple_of(s * chan, chan), chan), :] = total.astype(BF16)
        if keep:
            hid.ref[pl.ds(row, wide), :] = all_q
        high, low = split(total * w2)
        both = jnp.concatenate([high, low], axis=0).astype(BF16)
        sums = dot(both, group[...])
        sums = sums[0:chan] + sums[chan:]
        if cells > 128:
            sums = jnp.concatenate([sums, jnp.zeros((chan, cells - 128), F32)], axis=1)
        return part + pltpu.roll(sums, s * BRICK, 1)

    kept = (g, slope, hid) if keep else (g,)
    part = loop(slots.slots, step, jnp.zeros((chan, cells), F32), *kept)
    if keep:
        part_ref[...] = part
    else:
        spread_groups(slots.me, part, outs)


def slope_kernel(sign, make, s0, s1, s2, s3, x_ref, first, bias, slope, w1):
    slots = make((s0, s1, s2, s3))
    columns(first, bias, w1)
    hidden = first.shape[1]
    wide = BRICK * hidden

    def step(s, carry):
        _, e = slot_points(slots, s, x_ref)
        base = first_base(sign, e, w1)
        row = pl.multiple_of(s * wide, wide)
        for q in range(BRICK):
            _, gradient = gelu_pair(base + (sign * q) * w1[2])
            slope.ref[pl.ds(row + q * hidden, hidden), :] = gradient.astype(BF16)
        return carry

    loop(slots.slots, step, 0, slope)


def back_kernel(sign, weight, decode, make, s0, s1, s2, s3, x_ref, f_ref, second, *rest):
    slots = make((s0, s1, s2, s3))
    if decode:
        gp_ref, g, slope, hid, out_ref, dec_ref, dec = rest
        gp = gp_ref[...]
        dec[...] = jnp.zeros_like(dec)
    else:
        own_ref, recv_ref, g, slope, out_ref = rest
        gp = own_ref[...] + jnp.sum(recv_ref[...].astype(F32), axis=0)
    chan, hidden = second.shape
    wide = BRICK * hidden
    cells = gp.shape[1]
    w2 = second_layer(second)
    left_half = lax.broadcasted_iota(jnp.int32, (1, 2 * hidden), 1) < hidden

    def step(s, carry):
        acc, grad2 = carry
        at, e = slot_points(slots, s, x_ref)
        f = slot_source(slots, s, at, f_ref, weight)
        row = pl.multiple_of(s * wide, wide)
        gps = pltpu.roll(gp, cells - s * BRICK, 1)
        gs = g.ref[pl.ds(pl.multiple_of(s * chan, chan), chan), :].astype(F32)
        m = []
        for i in range(BRICK // 2):
            both = jnp.where(left_half, gps[:, 2 * i : 2 * i + 1], gps[:, 2 * i + 1 : 2 * i + 2])
            m.append(w2 * both)
            grad2 = grad2 + gs[:, 2 * i * hidden : 2 * (i + 1) * hidden] * both
        m = jnp.concatenate(m, axis=1)
        back = dot(jnp.transpose(m).astype(BF16), f)
        sum0 = jnp.zeros((hidden, BLOCK), F32)
        sum1 = jnp.zeros((hidden, BLOCK), F32)
        for q in range(BRICK):
            value = back[q * hidden : (q + 1) * hidden, :] * slope.ref[
                pl.ds(row + q * hidden, hidden), :
            ].astype(F32)
            sum0 = sum0 + value
            if q:
                sum1 = sum1 + float(q) * value
        scale = sign / RADIUS
        acc = (
            acc[0] + sum0 * (e[0] * scale),
            acc[1] + sum0 * (e[1] * scale),
            acc[2] + (sum0 * (e[2] * scale) + sum1 * scale),
            acc[3] + sum0,
        )
        if decode:
            value = dot(m.astype(BF16), hid.ref[pl.ds(row, wide), :])
            b = slots.block(s)
            dec[b] = dec[b] + value * slot_mask(slots, s, 1.0 / BRICK)
        return acc, grad2

    zero = jnp.zeros((hidden, BLOCK), F32)
    kept = (g, slope, hid) if decode else (g, slope)
    acc, grad2 = loop(
        slots.slots, step, ((zero,) * 4, jnp.zeros((chan, 2 * hidden), F32)), *kept
    )
    sums = [jnp.sum(a, axis=1, keepdims=True) for a in acc]
    packed = jnp.concatenate(sums + [jnp.zeros((hidden, 124), F32)], axis=1)
    out_ref[0:chan, :] = grad2[:, 0:hidden] + grad2[:, hidden : 2 * hidden]
    out_ref[chan : chan + 8, :] = jnp.transpose(packed)[0:8, :]
    if decode:
        for b in range(dec.shape[0]):
            dec_ref[:, b * BLOCK : (b + 1) * BLOCK] = dec[b].astype(BF16)


def sparse_factors(slots, planes_modes, part, lines, kx_ref, fj_ref):
    chan, cells = part.shape
    lanes = kx_ref.shape[1]
    planes = planes_modes // MODES
    iota = lax.broadcasted_iota(jnp.int32, (128, cells), 0).astype(F32)

    def hot(line):
        one = jnp.where(iota == line, 1.0, 0.0).astype(BF16)
        return jnp.concatenate([one, one], axis=0)

    plane = lax.broadcasted_iota(jnp.int32, (planes_modes, cells), 0)
    here = modulo(plane, planes).astype(F32) == lines[0]
    high, low = split(jnp.where(here, dot(fj_ref[...], hot(lines[1])), 0.0))
    left = jnp.concatenate([high, high, low], axis=1).astype(BF16)
    turned = jnp.transpose(jnp.concatenate([part, jnp.zeros((128 - chan, cells), F32)], axis=0))
    turned = turned[:, 0:chan]
    four = jnp.concatenate([turned] * (128 // chan), axis=1)
    value = dot(hot(lines[2]), kx_ref[...], TN) * jnp.concatenate([four] * (lanes // 128), axis=1)
    high, low = split(value)
    return left, jnp.concatenate([high, low, high], axis=0).astype(BF16)


def dense_kernel(subs, make, s0, s1, s2, s3, fk_ref, fj_ref, *rest):
    got, (x, lh, ll, perm, kx), (out_ref, *lats), (th, tl) = (
        rest[:subs], rest[subs : subs + 5], rest[subs + 5 : -2], rest[-2:]
    )
    slots = make((s0, s1, s2, s3))
    chan, planes, length = x.ref.shape[0:3]
    cells = got[0].shape[1]

    def plane(p, carry):
        rows = pl.ds(pl.multiple_of(p * length, length), length)
        x.wait(p)
        for group in range(chan // 4):
            a = jnp.concatenate([x.ref[4 * group + i, p] for i in range(4)], axis=1)
            t = dot(a, fk_ref[...])
            high, low = split(t[:, 0:128] + t[:, 128:256])
            th[rows, group * 128 : (group + 1) * 128] = high.astype(BF16)
            tl[rows, group * 128 : (group + 1) * 128] = low.astype(BF16)
        return carry

    lax.fori_loop(0, planes, plane, 0)
    lh.wait(0)
    ll.wait(0)
    count = out_ref.shape[0]
    for piece in range(4):
        cols = slice(piece * 256, (piece + 1) * 256)
        r = dot(lh.ref[...], th[:, cols]) + dot(lh.ref[...], tl[:, cols])
        high, low = split(r + dot(ll.ref[...], th[:, cols]))
        th[0:count, cols] = high.astype(BF16)
        tl[0:count, cols] = low.astype(BF16)
    part = got[0][...].astype(F32)
    for one in got[1:]:
        part = part + one[...].astype(F32)
    lines = slots.lines(slots.held)
    perm.wait(0)
    kx.wait(0)
    left, right = sparse_factors(slots, count, part, lines, kx.ref, fj_ref)
    moved = dot(th[0:count, :], perm.ref[...]) + dot(tl[0:count, :], perm.ref[...])
    out_ref[...] = (moved + dot(left, right)).astype(BF16)

    k = lax.broadcasted_iota(jnp.int32, (128, cells), 0)
    lane = lax.broadcasted_iota(jnp.int32, (128, cells), 1)
    total = dot(part.astype(BF16), same_cells(lines, lines), NT)
    for t in range(slots.slots):
        layer, row, column = slots.held(jnp.int32(t))
        first = pl.multiple_of(over(row, 16) * 16, 16)
        tile = x.ref[:, layer, pl.ds(first, 16), :].astype(F32)
        inside = lax.broadcasted_iota(jnp.int32, (1, 16, 128), 1) == row - first
        line = jnp.sum(jnp.where(inside, tile, 0.0), axis=1).astype(BF16)
        at = lane - t * BRICK
        hot = (k == column + at) & (at >= 0) & (at < BRICK)
        total = total + dot(line, jnp.where(hot, 1.0, 0.0).astype(BF16))
    spread_groups(slots.me, total.astype(BF16).astype(F32), lats)


def basis_kernel(rows_ref, kx_ref, ix_ref, fj_ref, bt):
    bt_ref = bt.ref
    rows, cells = bt_ref.shape
    width = 256
    piece = min(rows, 256)

    def place(i, carry):
        at = pl.ds(pl.multiple_of(i * width, width), width)
        lines = rows_ref[:, at]
        iota = lax.broadcasted_iota(jnp.int32, (128, width), 0).astype(F32)

        def hot(r):
            one = jnp.where(iota == lines[r : r + 1, :], 1.0, 0.0).astype(BF16)
            return jnp.concatenate([one, one], axis=0)

        tj = dot(fj_ref[...], hot(1))[0:1, :]
        hi, hk = hot(0), hot(2)
        for r in range(rows // piece):
            rs = slice(r * piece, (r + 1) * piece)
            value = dot(kx_ref[rs, :], hk) * (dot(ix_ref[rs, :], hi) * tj)
            bt_ref[rs, at] = value.astype(BF16)
        bt.start(i)
        return carry

    lax.fori_loop(0, cells // width, place, 0)


def send_cells(modes_rows, scale_row, bt, sy_ref, turned):
    bt_ref = bt.ref
    devices2, chan, cells = sy_ref.shape
    value = jnp.transpose(modes_rows)[0 : 2 * chan, :] * scale_row
    high, low = split(value)
    turned[...] = jnp.concatenate([high, low], axis=0).astype(BF16)
    per = max(1, 256 // cells)
    width = per * cells

    def step(i, carry):
        at = pl.ds(pl.multiple_of(i * width, width), width)
        o = dot(turned[...], bt_ref[:, at])
        o = (o[0 : 2 * chan] + o[2 * chan :]).astype(BF16)
        for j in range(per):
            for c in range(2):
                sy_ref[(i * per + j) * 2 + c] = o[
                    c * chan : (c + 1) * chan, j * cells : (j + 1) * cells
                ]
        return carry

    lax.fori_loop(0, devices2 // 2 // per, step, 0, unroll=2)


def block_mask():
    lane = over(lax.broadcasted_iota(jnp.int32, (8, 512), 1), 64)
    return jnp.where(lane == lax.broadcasted_iota(jnp.int32, (8, 512), 0), 1.0, 0.0)


def start_weights(core, w_ref, buffer, sems):
    own = buffer.shape[0]
    pieces = sems.shape[0]
    size = own // pieces
    copies = []
    for i in range(pieces):
        source = w_ref.at[pl.ds(core[0] * own + i * size, size)]
        copies.append(pltpu.make_async_copy(source, buffer.at[pl.ds(i * size, size)], sems.at[i]))
        copies[-1].start()
    return copies


def mix_kernel(
    core, recv_ref, fi_ref, scale_ref, w, bt,
    sy_ref, coef_ref, coef, mix, turned, w_ref, sems,
):
    copies = start_weights(core, w, w_ref, sems)
    number = coef.shape[0] // MODES
    chan = coef_ref.shape[0] // 2
    coef[...] = jnp.zeros_like(coef)
    mix[...] = jnp.zeros_like(mix)
    for c in range(2):
        if len(recv_ref.shape) == 4:
            got = recv_ref[:, c].astype(F32)
            got = got.reshape(got.shape[0] * got.shape[1], got.shape[2]).astype(BF16)
        else:
            got = recv_ref[c]
        x = dot(fi_ref[...], got)
        x = x[0:MODES] + x[MODES:]
        for n in range(number):
            coef[n * MODES : (n + 1) * MODES, c * chan : (c + 1) * chan] = x[
                :, n * chan : (n + 1) * chan
            ]
    coef_ref[...] = jnp.transpose(coef[...])[0 : 2 * chan, :]
    mask = block_mask()

    def one(n, carry):
        for group in range(MODES // 8):
            rows = pl.ds(pl.multiple_of(n * MODES + group * 8, 8), 8)
            c8 = coef[rows, :]
            c128 = c8 + pltpu.roll(c8, 64, 1)
            high, low = split(jnp.concatenate([c128] * 4, axis=1) * mask)
            left = jnp.concatenate([high, low], axis=0).astype(BF16)
            o = dot(left, w_ref[n, group * 8 : (group + 1) * 8].reshape(512, 64))
            mix[rows, 0:64] = o[0:8] + o[8:16]
        return carry

    for part, copy in enumerate(copies):
        copy.wait()
        each = number // len(copies)
        lax.fori_loop(part * each, (part + 1) * each, one, 0, unroll=4)
    bt.wait(0)
    send_cells(mix[...], scale_ref[...], bt, sy_ref, turned)


def mixback_kernel(
    core, recv_ref, column_ref, scale_ref, w, bt,
    sy_ref, gm_ref, gm, mix, turned, w_ref, sems, g_ref,
):
    bt_ref = bt.ref
    copies = start_weights(core, w, w_ref, sems)
    devices2, chan, cells = recv_ref.shape
    number = gm.shape[0] // MODES
    gm[...] = jnp.zeros_like(gm)

    def place(i, carry):
        at = pl.ds(pl.multiple_of(i * cells, cells), cells)
        for c in range(2):
            g_ref[c * chan : (c + 1) * chan, at] = recv_ref[2 * i + c]
        return carry

    lax.fori_loop(0, devices2 // 2, place, 0)
    bt.wait(0)
    gm[:, 0:64] = dot(bt_ref[...], g_ref[...], NT) * column_ref[...]
    gm_ref[...] = jnp.transpose(gm[...])[0:64, :]
    mask = block_mask()

    def one(n, carry):
        for group in range(MODES // 8):
            rows = pl.ds(pl.multiple_of(n * MODES + group * 8, 8), 8)
            high, low = split(gm[rows, 0:64])
            left = jnp.concatenate([high, low], axis=0).astype(BF16)
            o = dot(left, w_ref[n, group * 8 : (group + 1) * 8].reshape(512, 64), NT)
            o = (o[0:8] + o[8:16]) * mask
            o = (o[:, 0:128] + o[:, 128:256]) + (o[:, 256:384] + o[:, 384:512])
            mix[rows, :] = o + pltpu.roll(o, 64, 1)
        return carry

    for part, copy in enumerate(copies):
        copy.wait()
        each = number // len(copies)
        lax.fori_loop(part * each, (part + 1) * each, one, 0, unroll=2)
    send_cells(mix[...], scale_ref[...], bt, sy_ref, turned)


def point_kernel(subs, recv_ref, rg_ref, *rest):
    lats, (g_ref, b_ref) = rest[:subs], rest[subs:]
    preact = jnp.sum(recv_ref[...].astype(F32), axis=0)
    for one in lats:
        preact = preact + one[...].astype(F32)
    value, slope = gelu_pair(preact)
    b_ref[...] = value.astype(BF16).astype(F32)
    g = (slope * rg_ref[...]).astype(BF16)

    def copy(i, carry):
        g_ref[i] = g
        return carry

    lax.fori_loop(0, g_ref.shape[0], copy, 0)


def own_kernel(make, s0, s1, s2, s3, rows_ref, recv_ref, out_ref):
    slots = make((s0, s1, s2, s3))
    cells = out_ref.shape[1]
    mine = slots.lines(slots.own)
    total = jnp.zeros(out_ref.shape, F32)
    for u in range(slots.subs):
        source = slots.slab * slots.subs + u
        lines = rows_ref[:, pl.ds(pl.multiple_of(source * cells, cells), cells)]
        same = same_cells(mine, [lines[d : d + 1, :] for d in range(3)])
        total = total + dot(recv_ref[source * 2 + slots.core], same, NT)
    out_ref[...] = total


def outer_kernel(place, coef_ref, grad_ref, *rest):
    out_ref, left = rest[-2:]
    coef = coef_ref[...]
    grad = jnp.transpose(grad_ref[...])
    chan = coef.shape[0]
    lane = lax.broadcasted_iota(jnp.int32, (1, 256), 1)
    row = lax.broadcasted_iota(jnp.int32, (256, 256), 0)
    column = lax.broadcasted_iota(jnp.int32, (256, 256), 1)
    picked = modulo(row, 4) == over(column, 64)
    for chunk in range(coef.shape[1] // 64):
        part = coef[:, chunk * 64 : (chunk + 1) * 64]
        high, low = split(part)
        wide = jnp.concatenate([high, low, high, jnp.zeros_like(high)], axis=1)
        for x in range(16):
            left[x * chan : (x + 1) * chan, :] = jnp.where(
                over(modulo(lane, 64), 4) == x, wide, 0.0
            ).astype(BF16)
        g = grad[chunk * 64 : (chunk + 1) * 64, :]
        high, low = split(g)
        tall = jnp.concatenate([high, high, low, jnp.zeros_like(high)], axis=0)
        two = jnp.concatenate([tall, tall], axis=1)
        right = jnp.where(picked, jnp.concatenate([two, two], axis=1), 0.0).astype(BF16)
        o = dot(left[...], right).astype(BF16)
        for x in range(64):
            at = chunk * 64 + x
            out_ref[at // MODES, at % MODES] = o[
                (x // 4) * chan : (x // 4 + 1) * chan, (x % 4) * 64 : (x % 4 + 1) * 64
            ]


def tables(chan, planes, devices, count_j, count_k):
    count_i = planes * devices
    raw_i, norm_i = raw_basis(count_i)
    raw_j, norm_j = raw_basis(count_j)
    raw_k, norm_k = raw_basis(count_k)
    fk_high, fk_low = halves(raw_k * norm_k)
    fk = np.zeros((4, count_k, 2, 4, MODES), jnp.bfloat16)
    for c in range(4):
        fk[c, :, 0, c] = fk_high
        fk[c, :, 1, c] = fk_low
    fj_high, fj_low = halves(raw_j * norm_j)
    left = np.zeros((2, MODES, planes, planes, count_j), jnp.bfloat16)
    for p in range(planes):
        left[0, :, p, p] = fj_high.T
        left[1, :, p, p] = fj_low.T
    left = left.reshape(2, MODES * planes, planes * count_j)
    fi_high, fi_low = halves(raw_i * norm_i)
    fi = np.concatenate([fi_high.T, fi_low.T], axis=0)

    def expand(raw, order):
        high, low = halves(raw)
        both = np.concatenate([high.T, low.T], axis=1)
        return np.repeat(both, MODES, axis=0) if order == "rep" else np.tile(both, (MODES, 1))

    both = np.concatenate(halves(raw_k * norm_k), axis=0)
    kc = np.repeat(both, chan, axis=1)
    fj_both = np.concatenate([fj_high.T, fj_low.T], axis=1)
    fjp = np.repeat(fj_both, planes, axis=0)
    kx = expand(raw_k, "rep")
    ix = expand(raw_i, "tile")
    fj_rows = np.concatenate([h.T for h in halves(raw_j)], axis=1)
    norm_nl = np.repeat(norm_k, MODES) * np.tile(norm_i, MODES)
    return {
        "fk": fk.reshape(4 * count_k, 8 * MODES),
        "lh": left[0],
        "ll": left[1],
        "fi": fi,
        "kc": kc,
        "fjp": fjp,
        "kx": kx,
        "ix": ix,
        "fj": fj_rows,
        "norm_nl": norm_nl.astype(np.float32),
        "norm_j": norm_j.astype(np.float32),
    }


def permutation(chan):
    perm = np.zeros((chan, MODES, MODES, chan), jnp.bfloat16)
    for c in range(chan):
        for n in range(MODES):
            perm[c, n, n, c] = 1
    return perm.reshape(chan * MODES, MODES * chan)


def body(
    coords,
    features,
    valid_count,
    pair_block,
    pair_brick,
    pair_count,
    geometry,
    encoder_first,
    encoder_bias,
    encoder_second,
    decoder_first,
    decoder_bias,
    decoder_second,
    spectral,
    cotangent,
):
    subs = lax.axis_size("sub")
    devices = lax.axis_size("slab") * subs
    every = ("slab", "sub", "chan")
    slab_index = lax.axis_index("slab")
    sub_index = lax.axis_index("sub")
    chan_index = lax.axis_index("chan")
    pair = slab_index * subs + sub_index
    blocks_here = valid_count.shape[0]
    chan, planes, count_j, count_k = geometry.shape
    points = features.shape[0]
    hidden = encoder_first.shape[1]
    slots = subs * CAP
    cells = slots * BRICK
    all_cells = devices * cells
    own = spectral.shape[0] // 2
    rows = own * MODES
    split_n = MODES // own
    tab = {k: v if k.startswith("norm") else jnp.asarray(v) for k, v in
           tables(chan, planes, devices, count_j, count_k).items()}
    per_row = count_k // BRICK

    def place(values):
        return values // (count_j * per_row), values // per_row % count_j, values % per_row

    def make(refs):
        return Slots(refs, subs, planes, count_j, per_row)

    def shape(dims, kind=F32):
        return jax.ShapeDtypeStruct(dims, kind)

    def hold(*values):
        return lax.optimization_barrier(values)

    def ring(values, axis, size):
        moved = [values[0]]
        for k in range(1, size):
            moved.append(lax.ppermute(values[k], axis, [(i, (i + k) % size) for i in range(size)]))
        return moved

    scal = [(v, "scalar") for v in (pair_block, pair_brick, pair_count, valid_count)]
    features_t, cotangent_t = features.T, cotangent.T
    enc_layers = [encoder_first, encoder_bias[None], encoder_second.T]
    dec_layers = [decoder_first, decoder_bias[None], decoder_second.T]
    wide = BRICK * hidden
    by_slot = (max(1, slots // 4), 0)
    whole = "whole"
    w1_scratch = pltpu.VMEM((4, hidden, BLOCK), F32)
    hidden_shape = shape((slots * wide, BLOCK), BF16)
    values_shape = shape((chan, cells), BF16)

    def wholes(*arrays):
        return [(a, whole) for a in arrays]

    def net(sign, weight, keep, f, layers):
        outs = [(shape((slots * chan, wide), BF16), by_slot)]
        if keep:
            outs += [(hidden_shape, by_slot)] * 2 + [(shape((chan, cells)), whole)]
        else:
            outs += [(values_shape, whole)] * subs
        return call(
            functools.partial(net_kernel, sign, weight, keep, make),
            [*scal, *wholes(coords, f, *layers)], outs, [w1_scratch, pltpu.VMEM((wide, 128), BF16)],
        )

    with jax.named_scope("encoder_points"):
        enc_g, *message = net(1.0, QUADRATURE, False, features_t, enc_layers)
    with jax.named_scope("partial_exchange"):
        partials = ring(message, "sub", subs)

    slabs = devices // subs
    with jax.named_scope("slots_all"):
        pair_brick, _ = hold(pair_brick, message[0])
        around = jnp.stack(ring([pair_brick[0]] * slabs, "slab", slabs))
        bricks_all = jnp.take(around, (slab_index - jnp.arange(slabs)) % slabs, axis=0)
    lanes = chan * MODES
    with jax.named_scope("dense_transform"):
        dense, *latents = call(
            functools.partial(dense_kernel, subs, make),
            [*scal, *wholes(tab["fk"], tab["fjp"], *partials), (geometry, (planes, 1)),
             (tab["lh"], (1, 0)), (tab["ll"], (1, 0)), (jnp.asarray(permutation(chan)), (1, 0)),
             (tab["kc"], (1, 0))],
            [(shape((MODES * planes, lanes), BF16), whole), *[(values_shape, whole)] * subs],
            [pltpu.VMEM((planes * count_j, lanes), BF16)] * 2, 8e9, 1e7,
        )
    with jax.named_scope("dense_exchange"):
        dense = dense.reshape(MODES, planes, split_n, own * chan)
        dense = dense.transpose(0, 2, 1, 3).reshape(MODES * split_n, planes, own * chan)
        dense, pair = hold(dense, pair)
        dense = lax.all_to_all(dense, every, 0, 0, tiled=True)
        dense = dense.reshape(devices, 2, planes, own * chan)
        if planes % 8:
            dense = dense.transpose(1, 0, 2, 3).reshape(2, devices * planes, own * chan)
    with jax.named_scope("latent_exchange"):
        latents = ring(latents, "sub", subs)

    first_pair = (pair * 2 + chan_index) * own
    mode_j = first_pair // MODES
    kx = tab["kx"]
    norm_nl = jnp.asarray(tab["norm_nl"])
    if split_n > 1:
        begin = first_pair % MODES * MODES
        kx = lax.dynamic_slice_in_dim(kx, begin, rows, 0)
        norm_nl = lax.dynamic_slice_in_dim(norm_nl, begin, rows, 0)
    scale = norm_nl * lax.dynamic_index_in_dim(jnp.asarray(tab["norm_j"]), mode_j, 0, keepdims=False)
    scale_column, scale_row = scale[:, None], scale[None, :]
    fj = lax.dynamic_slice_in_dim(tab["fj"], mode_j, 1, 0)
    fj = jnp.broadcast_to(fj, (16, fj.shape[1]))
    layer, row, column = place(bricks_all)
    slab_of = jnp.arange(slabs, dtype=jnp.int32)[:, None, None, None]
    owner = jnp.arange(subs, dtype=jnp.int32)[None, None, :, None]
    plane = (slab_of * subs + owner) * planes + layer
    lines = jnp.stack([plane.reshape(-1), row.reshape(-1), column.reshape(-1) * BRICK])
    lines = jnp.repeat(lines, BRICK, axis=1)
    inner = jnp.arange(all_cells, dtype=jnp.int32) % BRICK
    rows_all = (lines + jnp.stack([0 * inner, 0 * inner, inner])).astype(F32)

    with jax.named_scope("cell_basis"):
        (bt,) = call(
            basis_kernel,
            wholes(rows_all, kx, tab["ix"][:rows], fj),
            [(shape((rows, all_cells), BF16), (all_cells // 256, 1))], [], 5e9, 8e6,
        )

    readers = shape((2 * devices, chan, cells), BF16)
    by_mode = shape((2 * chan, rows))
    mode_scratch = [
        pltpu.VMEM((rows, 128), F32),
        pltpu.VMEM((rows, 128), F32),
        pltpu.VMEM((4 * chan, rows), BF16),
        pltpu.VMEM((own, MODES, 2 * chan, 2 * chan), BF16),
        pltpu.SemaphoreType.DMA((min(8, own),)),
    ]
    core = chan_index.astype(jnp.int32).reshape(1)
    with jax.named_scope("mix"):
        bt, *latents = hold(bt, *latents)
        sent, coefficient = call(
            mix_kernel,
            [(core, "scalar"), *wholes(dense, tab["fi"], scale_row), (spectral, "raw"), (bt, (1, 0))],
            [(readers, whole), (by_mode, whole)], mode_scratch, 4e9, 2e7,
        )
    with jax.named_scope("preact_exchange"):
        arrived = lax.all_to_all(sent, every, 0, 0, tiled=True)
    swap = [(0, 1), (1, 0)]
    with jax.named_scope("coefficient_swap"):
        coef_near = lax.dynamic_slice_in_dim(coefficient, chan_index * chan, chan, 0)
        coef_sent = lax.dynamic_slice_in_dim(coefficient, (1 - chan_index) * chan, chan, 0)
        coef_far = lax.ppermute(coef_sent, "chan", swap)

    with jax.named_scope("decoder_points"):
        cotangent_t, _ = hold(cotangent_t, sent)
        dec_g, dec_slope, dec_hid, read_grads = net(
            -1.0, 1.0 / BRICK, True, cotangent_t, dec_layers
        )

    with jax.named_scope("cell_values"):
        arrived, read_grads, coef_far = hold(arrived, read_grads, coef_far)
        cell_grads, bricks = call(
            functools.partial(point_kernel, subs),
            wholes(arrived, read_grads, *latents),
            [(readers, whole), (shape((chan, cells)), whole)], [], 1e6, 1e6,
        )
    with jax.named_scope("cell_grads_all"):
        all_grads = lax.all_to_all(cell_grads, every, 0, 0, tiled=True)

    def back(sign, weight, decode, f, layers, operands, saved):
        outs = [(shape((chan + 8, hidden)), whole)]
        scratch = []
        if decode:
            outs.append((shape((chan, points), BF16), whole))
            scratch.append(pltpu.VMEM((blocks_here, chan, BLOCK), F32))
        return call(
            functools.partial(back_kernel, sign, weight, decode, make),
            [*scal, *wholes(coords, f, layers[2], *operands),
             *[(v, by_slot) for v in saved]],
            outs, scratch,
        )

    with jax.named_scope("decoder_back"):
        dec_grads, decoded = back(
            -1.0, 1.0 / BRICK, True, cotangent_t, dec_layers, [bricks],
            [dec_g, dec_slope, dec_hid],
        )

    with jax.named_scope("encoder_slope"):
        slope_coords, _ = hold(coords, cell_grads)
        (enc_slope,) = call(
            functools.partial(slope_kernel, 1.0, make),
            [*scal, *wholes(slope_coords, *enc_layers[0:2])],
            [(hidden_shape, by_slot)], [w1_scratch], 1e9, 4e6,
        )
    with jax.named_scope("mix_back"):
        all_grads, decoded, enc_slope = hold(all_grads, decoded, enc_slope)
        sent_back, grad_modes = call(
            mixback_kernel,
            [(core, "scalar"), *wholes(all_grads, scale_column, scale_row), (spectral, "raw"),
             (bt, (1, 0))],
            [(readers, whole), (by_mode, whole)],
            mode_scratch + [pltpu.VMEM((2 * chan, all_cells), BF16)], 4e9, 2e7,
        )
    with jax.named_scope("latent_grad_exchange"):
        arrived_back = lax.all_to_all(sent_back, every, 0, 0, tiled=True)
    with jax.named_scope("grad_swap"):
        grad_far = lax.ppermute(grad_modes, "chan", swap)
    with jax.named_scope("own_cells"):
        (own_grads,) = call(
            functools.partial(own_kernel, make),
            [*scal, *wholes(rows_all, all_grads)],
            [(shape((chan, cells)), whole)], [], 1e8, 1e6,
        )

    with jax.named_scope("grad_spectral"):
        block_n = min(8, own)
        steps = own // block_n
        width = block_n * MODES

        def lanes_spec(height):
            return pl.BlockSpec((height, width), lambda n, place: (0, n))

        def outer(half, coef, grad, held):
            more = [] if held is None else [held]
            return pl.pallas_call(
                outer_kernel,
                grid_spec=pltpu.PrefetchScalarGridSpec(
                    num_scalar_prefetch=1,
                    grid=(steps,),
                    in_specs=[lanes_spec(chan), lanes_spec(2 * chan)]
                    + [pl.BlockSpec(memory_space=pl.ANY)] * len(more),
                    out_specs=pl.BlockSpec(
                        (block_n, MODES, chan, 2 * chan),
                        lambda n, place: (place[0] * steps + n, 0, 0, 0),
                    ),
                    scratch_shapes=[pltpu.VMEM((16 * chan, 256), BF16)],
                ),
                out_shape=shape((2 * own, MODES, chan, 2 * chan), BF16),
                input_output_aliases={3: 0} if more else {},
                compiler_params=pltpu.CompilerParams(vmem_limit_bytes=VMEM_LIMIT),
                cost_estimate=pl.CostEstimate(
                    flops=10**7, bytes_accessed=10**7, transcendentals=0
                ),
            )(half, coef, grad, *more)

        grad_spectral = outer(core, coef_near, grad_modes, None)

    with jax.named_scope("encoder_back"):
        arrived_back, own_grads, grad_spectral = hold(arrived_back, own_grads, grad_spectral)
        (enc_grads,) = back(
            1.0, QUADRATURE, False, features_t, enc_layers, [own_grads, arrived_back],
            [enc_g, enc_slope],
        )
    with jax.named_scope("grad_spectral_far"):
        grad_far, _ = hold(grad_far, enc_grads)
        grad_spectral = outer(1 - core, coef_far, grad_far, grad_spectral)
    with jax.named_scope("weight_sums"):
        both = jnp.concatenate([enc_grads, dec_grads], axis=1).astype(BF16)
        spread = jnp.broadcast_to(both[None], (devices,) + both.shape)
        total = jnp.sum(
            lax.all_to_all(spread, ("slab", "sub"), 0, 0, tiled=True).astype(F32), axis=0
        )
        small = total[chan:]
        small = small + lax.ppermute(small, "chan", swap)
    enc_second = total[:chan, :hidden].T
    dec_second = total[:chan, hidden:].T
    return (
        decoded.T,
        small[0:3, :hidden],
        small[3, :hidden],
        enc_second,
        small[0:3, hidden:],
        small[3, hidden:],
        dec_second,
        grad_spectral,
    )


def solution(mesh):
    placed = (
        P(None, ("groups", "slab", "sub")),
        P(("groups", "slab", "sub"), "chan"),
        P(("groups", "slab", "sub")),
        P(("groups", "slab"), None, None, None),
        P(("groups", "slab"), None, None, None),
        P(("groups", "slab"), None, None),
        P("chan", ("groups", "slab", "sub"), None, None),
        P(),
        P(),
        P(None, "chan"),
        P(),
        P(),
        P(None, "chan"),
        P(("slab", "sub"), None, None, None),
        P(("groups", "slab", "sub"), "chan"),
    )
    return jax.shard_map(
        body,
        mesh=mesh,
        in_specs=placed,
        out_specs=(
            P(("groups", "slab", "sub"), "chan"),
            P("groups", None),
            P("groups"),
            P("groups", "chan"),
            P("groups", None),
            P("groups"),
            P("groups", "chan"),
            P(("groups", "slab", "sub"), None, "chan", None),
        ),
        check_vma=False,
    )
```

time: 183 us -> 156 us (0.85)
  blocking collectives: 33.5 us -> 0 us
  local copies, waits for them, and re-layouts: 37.8 us -> 12.8 us
  starting transfers between devices: 21.5 us -> 38.9 us
  Pallas kernels: 82.8 us -> 91.6 us
  waiting for transfers between devices: 3.75 us -> 6.84 us
  other arithmetic: 1.03 us -> 3.64 us
    all_to_all x2 -> x0, blocking collectives: 31.5 us -> none  [the longest x1 16.2 us: body(): all_grads = lax.all_to_all(cell_grads, every, 0, 0, tiled=True)]
    unnamed x72 -> x34, local copies, waits for them, and re-layouts: 31.1 us -> 4.39 us
    ppermute x0 -> x9, starting transfers between devices: none -> 15.3 us  [ring(): lax.ppermute(values[k], axis, [(i, (i + k) % size) for i in range(size)])]
    pallas_call x11 -> x13, Pallas kernels: 82.8 us -> 91.6 us  [the longest x11 78 us: call(): pl.pallas_call(wrapped, out_shape=[jax.ShapeDtypeStruct(o.shape, o.dtype)...]
    all_to_all x1, starting transfers between devices: 2.59 us -> 5.85 us  [body(): arrived_back = lax.all_to_all(sent_back, every, 0, 0, tiled=True)]
    all_to_all x1, starting transfers between devices: 2.6 us -> 4.79 us  [body(): dense = lax.all_to_all(dense, every, 0, 0, tiled=True)]
    all_gather x1 -> x0, blocking collectives: 2.08 us -> none  [body(): gathered = lax.all_gather(near, 'chan', axis=0)]
  transfers between devices with their start and end apart: 8 -> 17, of which waited for: 3 -> 6; matrix products, arithmetic and copies ran while one was open for 3% -> 6% of each run, Pallas kernels for 22% -> 26%
where the time goes in v1:
time: 156 us; the launch traced here: 155 us
  Pallas kernels  91.6 us (59%)
  starting transfers between devices  38.9 us (25%)
  local copies, waits for them, and re-layouts  12.8 us (8%)
  waiting for transfers between devices  6.84 us (4%)
  other arithmetic  3.64 us (2%)
    pallas_call x11, Pallas kernels, call(): pl.pallas_call(wrapped, out_shape=[jax.ShapeDtypeStruct(o.shape, o.dtype)...  78 us
    ppermute x9, starting transfers between devices, ring(): lax.ppermute(values[k], axis, [(i, (i + k) % size) for i in range(size)])  15.3 us
    pallas_call x2, Pallas kernels, outer(): pl.pallas_call(outer_kernel, grid_spec=pltpu.PrefetchScalarGridSpec(num_s...  13.7 us
    all_to_all x1, starting transfers between devices, body(): arrived_back = lax.all_to_all(sent_back, every, 0, 0, tiled=True)  5.85 us
    all_to_all x1, starting transfers between devices, body(): lax.all_to_all(spread, ('slab', 'sub'), 0, 0, tiled=True).astype(F32)  5.27 us
    all_to_all x1, starting transfers between devices, body(): dense = lax.all_to_all(dense, every, 0, 0, tiled=True)  4.79 us
    unnamed x34, local copies, waits for them, and re-layouts  4.39 us
    all_to_all x1, starting transfers between devices, body(): all_grads = lax.all_to_all(cell_grads, every, 0, 0, tiled=True)  4.08 us
  transfers between devices with their start and end apart: 17, of which 6 were waited for; matrix products, arithmetic and copies ran while one was open for 6% of the time, Pallas kernels for 26%

profile of v1, /device:TPU:0, one launch (start us, length us, event | category | flops | bytes accessed | tf_op | source)
XLA Modules:
  0.0 154.9 jit_solution(14209330221381463426)
XLA Ops:
  0.6 5.8 %encoder_points.1 = (bf16[512,512]{1,0:T(8,128)(2,1)}, bf16[32,128]{1,0:T(8,128)(2,1)}, bf16[32,128]{1,0:T(8,128)(2,1)}, bf16[32,128]{1,0:T(8,128)(2,1)}, bf16[32,128]{1,0:T(8,128)(2,1)}) custom-call(s32[1,4,4,4]{3,2,1,0:T(4,128)} %refs_0_.13, s32[1,4,4,4]{3,2,1,0:T(4,128)} %refs_1_.14, s32[1,4,4]{2,1,0:T(4,128)} %refs_2_.15, s32[8]{0:T(128)} %refs_3_.13, ...), custom_call_target="tpu_custom_call" | custom-call | flops 1000000000 | bytes 8000000 | tf_op jit(solution)/shard_map/encoder_points/pallas_call | solution.py:150
  6.4 5.1 %collective-permute-start.5 = (s32[4,4,4]{2,1,0:T(4,128)}, s32[4,4,4]{2,1,0:T(4,128)S(1)}, u32[]{:S(2)}, u32[]{:S(2)}) collective-permute-start(s32[4,4,4]{2,1,0:T(4,128)} %bitcast.34), channel_id=1, source_target_pairs={{0,24},{8,0},{16,8},{24,16},{1,25},{9,1},{17,9},{25,17},{2,26},{10... | collective-permute-start | bytes 776 | tf_op jit(solution)/shard_map/slots_all/ppermute | solution.py:802
  11.6 1.0 collective-permute-start.3
  12.6 1.5 collective-permute-start
  14.1 1.5 collective-permute-start.1
  15.9 1.5 collective-permute-start.2
  17.4 0.7 pad_add_fusion
  20.0 0.6 copy-done.15
  20.6 12.4 %dense_transform.1 = (bf16[256,1024]{1,0:T(8,128)(2,1)}, bf16[32,128]{1,0:T(8,128)(2,1)}, bf16[32,128]{1,0:T(8,128)(2,1)}, bf16[32,128]{1,0:T(8,128)(2,1)}, bf16[32,128]{1,0:T(8,128)(2,1)}) custom-call(s32[1,4,4,4]{3,2,1,0:T(4,128)} %refs_0_.13, s32[1,4,4,4]{3,2,1,0:T(4,128)} %refs_1_.14, s32[1,4,4]{2,1,0:T(4,128)} %refs_2_.15, s32[8]{0:T(128)} %refs_3_.13, ...), custom_call_target="tpu_custom_call" | custom-call | flops 8000000000 | bytes 10000000 | tf_op jit(solution)/shard_map/dense_transform/pallas_call | solution.py:150
  33.0 4.8 %all-to-all-start = ((bf16[32,8,1024]{2,1,0:T(8,128)(2,1)}), bf16[32,8,1024]{2,1,0:T(8,128)(2,1)S(1)}, u32[]{:S(2)}, u32[]{:S(2)}) async-start(bf16[32,8,1024]{2,1,0:T(8,128)(2,1)} %bitcast.28), calls=%async_computation | async-start | bytes 1048576 | tf_op jit(solution)/shard_map/dense_exchange/all_to_all | solution.py:854
  37.8 0.6 add_convert_fusion.refs_0_.refs_4_
  38.4 1.8 %collective-permute-start.6 = (bf16[32,128]{1,0:T(8,128)(2,1)}, bf16[32,128]{1,0:T(8,128)(2,1)S(1)}, u32[]{:S(2)}, u32[]{:S(2)}) collective-permute-start(bf16[32,128]{1,0:T(8,128)(2,1)} %get-tuple-element.59), channel_id=1, source_target_pairs={{0,2},{2,4},{4,6},{6,0},{1,3},{3,5},{5,7},{7,1},{8,10},{10,12},{12... | collective-permute-start | bytes 24584 | tf_op jit(solution)/shard_map/latent_exchange/ppermute | solution.py:802
  40.1 1.5 collective-permute-start.7
  41.6 1.5 collective-permute-start.8
  43.7 0.7 dynamic-slice_reduce_fusion
  44.4 0.6 broadcast_in_dim.46.refs_3_
  45.0 5.8 %cell_basis.1.refs_5_ = bf16[1024,2048]{1,0:T(8,128)(2,1)} custom-call(f32[3,2048]{1,0:T(4,128)} %add_convert_fusion.refs_0_.refs_4_, bf16[1024,256]{1,0:T(8,128)(2,1)} %constant.166.clone.refs_1_, bf16[1024,256]{1,0:T(8,128)(2,1)} %constant.167.clone.refs_2_, bf16[16,256]{1,0:T(8,128)(2,1)} %broadcast_in_dim.46.refs_3_), custom_call_target="tpu_custom_call" | custom-call | flops 5000000000 | bytes 8000000 | tf_op jit(solution)/shard_map/cell_basis/pallas_call | solution.py:150
  50.8 1.2 broadcast_multiply_fusion
  52.1 1.2 all-to-all-done
  53.3 0.8 copy-done
  54.1 10.2 %mix.1 = (bf16[32,32,128]{2,1,0:T(8,128)(2,1)}, f32[64,1024]{1,0:T(8,128)}) custom-call(s32[1]{0:T(128)} %bitcast.refs_0_.place, bf16[16,2,8,1024]{3,2,1,0:T(8,128)(2,1)} %bitcast.27, bf16[64,128]{1,0:T(8,128)(2,1)} %constant.163.clone.refs_2_, f32[1,1024]{1,0:T(1,128)} %bitcast.31, bf16[64,32,64,64]{3,2,1,0:T(8,128)(2,1)} %refs_4_.12, ...), custom_call_target="tpu_custom_call" | custom-call | flops 4000000000 | bytes 20000000 | tf_op jit(solution)/shard_map/mix/pallas_call | solution.py:150
  64.4 3.3 %all-to-all-start.1 = ((bf16[32,32,128]{2,1,0:T(8,128)(2,1)}), bf16[32,32,128]{2,1,0:T(8,128)(2,1)S(1)}, u32[]{:S(2)}, u32[]{:S(2)}) async-start(bf16[32,32,128]{2,1,0:T(8,128)(2,1)} %get-tuple-element.63), calls=%async_computation.1 | async-start | bytes 524288 | tf_op jit(solution)/shard_map/preact_exchange/all_to_all | solution.py:907
  67.6 1.6 %constant_dynamic-slice_fusion = (f32[32,1024]{1,0:T(8,128)}, f32[32,1024]{1,0:T(8,128)S(1)}) fusion(f32[64,1024]{1,0:T(8,128)} %get-tuple-element.66, s32[]{:T(128)S(6)} %select_n.146, s32[]{:T(128)S(6)} %select_n.145), kind=kLoop, calls=%fused_computation.37 | loop fusion | bytes 524296 | tf_op jit(solution)/shard_map/coefficient_swap/dynamic_slice | solution.py:910
  69.3 6.9 %decoder_points.1 = (bf16[512,512]{1,0:T(8,128)(2,1)}, bf16[8192,128]{1,0:T(8,128)(2,1)}, bf16[8192,128]{1,0:T(8,128)(2,1)}, f32[32,128]{1,0:T(8,128)}) custom-call(s32[1,4,4,4]{3,2,1,0:T(4,128)} %refs_0_.13, s32[1,4,4,4]{3,2,1,0:T(4,128)} %refs_1_.14, s32[1,4,4]{2,1,0:T(4,128)} %refs_2_.15, s32[8]{0:T(128)} %refs_3_.13, f32[3,1024]{1,0:T(4,128)} %refs_4_.13, ...), custom_call_target="tpu_custom_call" | custom-call | flops 1000000000 | bytes 8000000 | tf_op jit(solution)/shard_map/decoder_points/pallas_call | solution.py:150
  76.3 1.7 %all-to-all-done.1.refs_0_ = bf16[32,32,128]{2,1,0:T(8,128)(2,1)S(1)} async-done(((bf16[32,32,128]{2,1,0:T(8,128)(2,1)}), bf16[32,32,128]{2,1,0:T(8,128)(2,1)S(1)}, u32[]{:S(2)}, u32[]{:S(2)}) %all-to-all-start.1) | async-done | bytes 262176 | tf_op jit(solution)/shard_map/preact_exchange/all_to_all | solution.py:907
  78.0 0.7 copy-done.2
  78.7 2.0 %cell_values.1 = (bf16[32,32,128]{2,1,0:T(8,128)(2,1)}, f32[32,128]{1,0:T(8,128)}) custom-call(bf16[32,32,128]{2,1,0:T(8,128)(2,1)} %copy-done.2, f32[32,128]{1,0:T(8,128)} %get-tuple-element.68.refs_1_, bf16[32,128]{1,0:T(8,128)(2,1)} %get-tuple-element.69.refs_2_, bf16[32,128]{1,0:T(8,128)(2,1)} %copy-done.9, bf16[32,128]{1,0:T(8,128)(2,1)} %copy-done.10, ...), custom_call_target="tpu_custom_call" | custom-call | flops 1000000 | bytes 1000000 | tf_op jit(solution)/shard_map/cell_values/pallas_call | solution.py:150
  80.7 4.1 %all-to-all-start.2 = ((bf16[32,32,128]{2,1,0:T(8,128)(2,1)}), bf16[32,32,128]{2,1,0:T(8,128)(2,1)S(1)}, u32[]{:S(2)}, u32[]{:S(2)}) async-start(bf16[32,32,128]{2,1,0:T(8,128)(2,1)} %get-tuple-element.73), calls=%async_computation.2 | async-start | bytes 524288 | tf_op jit(solution)/shard_map/cell_grads_all/all_to_all | solution.py:928
  84.9 1.1 copy.37.refs_2_
  85.9 4.8 %encoder_slope.1.refs_10_ = bf16[8192,128]{1,0:T(8,128)(2,1)} custom-call(s32[1,4,4,4]{3,2,1,0:T(4,128)} %refs_0_.13, s32[1,4,4,4]{3,2,1,0:T(4,128)} %refs_1_.14, s32[1,4,4]{2,1,0:T(4,128)} %refs_2_.15, s32[8]{0:T(128)} %refs_3_.13, f32[3,1024]{1,0:T(4,128)} %refs_4_.13, f32[3,64]{1,0:T(4,128)} %refs_5_.2, f32[1,64]{1,0:T(1,128)} %bitcast.49), custom_call_target="tpu_custom_call" | custom-call | flops 1000000000 | bytes 4000000 | tf_op jit(solution)/shard_map/encoder_slope/pallas_call | solution.py:150
  90.7 7.4 %decoder_back.1 = (f32[40,64]{1,0:T(8,128)}, bf16[32,1024]{1,0:T(8,128)(2,1)}) custom-call(s32[1,4,4,4]{3,2,1,0:T(4,128)} %refs_0_.13, s32[1,4,4,4]{3,2,1,0:T(4,128)} %refs_1_.14, s32[1,4,4]{2,1,0:T(4,128)} %refs_2_.15, s32[8]{0:T(128)} %refs_3_.13, f32[3,1024]{1,0:T(4,128)} %refs_4_.13, bf16[32,1024]{1,0:T(8,128)(2,1)} %bitcast.30, f32[32,64]{1,0:T(8,128)} %bitcast.38, ...), custom_call_target="tpu_custom_call" | custom-call | flops 1000000000 | bytes 8000000 | tf_op jit(solution)/shard_map/decoder_back/pallas_call | solution.py:150
  98.1 0.7 copy-done.1
  98.8 13.5 %mix_back.1 = (bf16[32,32,128]{2,1,0:T(8,128)(2,1)}, f32[64,1024]{1,0:T(8,128)}) custom-call(s32[1]{0:T(128)} %bitcast.refs_0_.place, bf16[32,32,128]{2,1,0:T(8,128)(2,1)} %copy-done.1, f32[1024,1]{1,0:T(8,128)} %copy.37.refs_2_, f32[1,1024]{1,0:T(1,128)} %bitcast.32, bf16[64,32,64,64]{3,2,1,0:T(8,128)(2,1)} %refs_4_.12, bf16[1024,2048]{1,0:T(8,128)(2,1)} %cell_basis.1.refs_5_), custom_call_target="tpu_custom_call" | custom-call | flops 4000000000 | bytes 20000000 | tf_op jit(solution)/shard_map/mix_back/pallas_call | solution.py:150
  112.3 5.8 %all-to-all-start.3 = ((bf16[32,32,128]{2,1,0:T(8,128)(2,1)}), bf16[32,32,128]{2,1,0:T(8,128)(2,1)S(1)}, u32[]{:S(2)}, u32[]{:S(2)}) async-start(bf16[32,32,128]{2,1,0:T(8,128)(2,1)} %get-tuple-element.82), calls=%async_computation.3 | async-start | bytes 524288 | tf_op jit(solution)/shard_map/latent_grad_exchange/all_to_all | solution.py:966
  118.2 6.8 %grad_spectral.1.rest_0_ = bf16[64,32,32,64]{3,2,1,0:T(8,128)(2,1)} custom-call(s32[1]{0:T(128)} %bitcast.refs_0_.place, f32[32,1024]{1,0:T(8,128)} %get-tuple-element.94.coef_ref, f32[64,1024]{1,0:T(8,128)} %get-tuple-element.83.grad_ref), custom_call_target="tpu_custom_call" | custom-call | flops 10000000 | bytes 10000000 | tf_op jit(solution)/shard_map/grad_spectral/pallas_call | solution.py:986
  125.1 2.1 %own_cells.1.refs_7_ = f32[32,128]{1,0:T(8,128)} custom-call(s32[1,4,4,4]{3,2,1,0:T(4,128)} %refs_0_.13, s32[1,4,4,4]{3,2,1,0:T(4,128)} %refs_1_.14, s32[1,4,4]{2,1,0:T(4,128)} %refs_2_.15, s32[8]{0:T(128)} %refs_3_.13, f32[3,2048]{1,0:T(4,128)} %add_convert_fusion.refs_0_.refs_4_, bf16[32,32,128]{2,1,0:T(8,128)(2,1)} %copy-done.1), custom_call_target="tpu_custom_call" | custom-call | flops 100000000 | bytes 1000000 | tf_op jit(solution)/shard_map/own_cells/pallas_call | solution.py:150
  127.2 1.6 %all-to-all-done.3.refs_8_ = bf16[32,32,128]{2,1,0:T(8,128)(2,1)S(1)} async-done(((bf16[32,32,128]{2,1,0:T(8,128)(2,1)}), bf16[32,32,128]{2,1,0:T(8,128)(2,1)S(1)}, u32[]{:S(2)}, u32[]{:S(2)}) %all-to-all-start.3) | async-done | bytes 262176 | tf_op jit(solution)/shard_map/latent_grad_exchange/all_to_all | solution.py:966
  128.8 0.7 copy-done.5
  129.5 7.0 %encoder_back.1 = f32[40,64]{1,0:T(8,128)} custom-call(s32[1,4,4,4]{3,2,1,0:T(4,128)} %refs_0_.13, s32[1,4,4,4]{3,2,1,0:T(4,128)} %refs_1_.14, s32[1,4,4]{2,1,0:T(4,128)} %refs_2_.15, s32[8]{0:T(128)} %refs_3_.13, f32[3,1024]{1,0:T(4,128)} %refs_4_.13, bf16[32,1024]{1,0:T(8,128)(2,1)} %bitcast.43, f32[32,64]{1,0:T(8,128)} %bitcast.46, ...), custom_call_target="tpu_custom_call" | custom-call | flops 1000000000 | bytes 8000000 | tf_op jit(solution)/shard_map/encoder_back/pallas_call | solution.py:150
  136.5 0.7 convert.6
  137.3 0.7 broadcast_in_dim.49
  138.0 5.3 %all-to-all-start.4 = ((bf16[16,40,128]{2,1,0:T(8,128)(2,1)}), bf16[16,40,128]{2,1,0:T(8,128)(2,1)S(1)}, u32[]{:S(2)}, u32[]{:S(2)}) async-start(bf16[16,40,128]{2,1,0:T(8,128)(2,1)} %broadcast_in_dim.49), calls=%async_computation.4 | async-start | bytes 327680 | tf_op jit(solution)/shard_map/weight_sums/all_to_all | solution.py:1022
  143.4 1.5 collective-permute-done.11.grad_ref
  144.9 0.7 copy-done.4
  145.6 6.8 %grad_spectral_far.1 = bf16[64,32,32,64]{3,2,1,0:T(8,128)(2,1)} custom-call(s32[1]{0:T(128)S(6)} %sub.47.place, f32[32,1024]{1,0:T(8,128)} %copy-done.6, f32[64,1024]{1,0:T(8,128)} %copy-done.4, bf16[64,32,32,64]{3,2,1,0:T(8,128)(2,1)} %grad_spectral.1.rest_0_), custom_call_target="tpu_custom_call", output_to_operand_aliasing={{}: (3, {})} | custom-call | flops 10000000 | bytes 10000000 | tf_op jit(solution)/shard_map/grad_spectral_far/pallas_call | solution.py:986
  152.7 0.7 slice_bitcast_fusion
  153.7 0.6 slice_bitcast_fusion.2
  154.3 0.7 fusion.6
  (67 shorter events, 3.6 us)
Async XLA Ops:
  6.4 9.5 %collective-permute-start.5 = (s32[4,4,4]{2,1,0:T(4,128)}, s32[4,4,4]{2,1,0:T(4,128)S(1)}, u32[]{:S(2)}, u32[]{:S(2)}) collective-permute-start(s32[4,4,4]{2,1,0:T(4,128)} %bitcast.34), channel_id=1, source_target_pairs={{0,24},{8,0},{16,8},{24,16},{1,25},{9,1},{17,9},{25,17},{2,26},{10... | collective-permute-start | bytes 776 | tf_op jit(solution)/shard_map/slots_all/ppermute | solution.py:802
  11.5 5.9 %collective-permute-start.4 = (s32[4,4,4]{2,1,0:T(4,128)}, s32[4,4,4]{2,1,0:T(4,128)S(1)}, u32[]{:S(2)}, u32[]{:S(2)}) collective-permute-start(s32[4,4,4]{2,1,0:T(4,128)} %bitcast.35), channel_id=1, source_target_pairs={{0,16},{8,24},{16,0},{24,8},{1,17},{9,25},{17,1},{25,9},{2,18},{10... | collective-permute-start | bytes 776 | tf_op jit(solution)/shard_map/slots_all/ppermute | solution.py:802
  11.6 5.9 %collective-permute-start.3 = (s32[4,4,4]{2,1,0:T(4,128)}, s32[4,4,4]{2,1,0:T(4,128)S(1)}, u32[]{:S(2)}, u32[]{:S(2)}) collective-permute-start(s32[4,4,4]{2,1,0:T(4,128)} %bitcast.36), channel_id=1, source_target_pairs={{0,8},{8,16},{16,24},{24,0},{1,9},{9,17},{17,25},{25,1},{2,10},{10... | collective-permute-start | bytes 776 | tf_op jit(solution)/shard_map/slots_all/ppermute | solution.py:802
  12.6 6.8 %collective-permute-start = (bf16[32,128]{1,0:T(8,128)(2,1)}, bf16[32,128]{1,0:T(8,128)(2,1)S(1)}, u32[]{:S(2)}, u32[]{:S(2)}) collective-permute-start(bf16[32,128]{1,0:T(8,128)(2,1)} %get-tuple-element.51), channel_id=1, source_target_pairs={{0,2},{2,4},{4,6},{6,0},{1,3},{3,5},{5,7},{7,1},{8,10},{10,12},{12... | collective-permute-start | bytes 24584 | tf_op jit(solution)/shard_map/partial_exchange/ppermute | solution.py:802
  14.1 5.3 %collective-permute-start.1 = (bf16[32,128]{1,0:T(8,128)(2,1)}, bf16[32,128]{1,0:T(8,128)(2,1)S(1)}, u32[]{:S(2)}, u32[]{:S(2)}) collective-permute-start(bf16[32,128]{1,0:T(8,128)(2,1)} %get-tuple-element.52), channel_id=1, source_target_pairs={{0,4},{2,6},{4,0},{6,2},{1,5},{3,7},{5,1},{7,3},{8,12},{10,14},{12... | collective-permute-start | bytes 24584 | tf_op jit(solution)/shard_map/partial_exchange/ppermute | solution.py:802
  15.9 3.9 %collective-permute-start.2 = (bf16[32,128]{1,0:T(8,128)(2,1)}, bf16[32,128]{1,0:T(8,128)(2,1)S(1)}, u32[]{:S(2)}, u32[]{:S(2)}) collective-permute-start(bf16[32,128]{1,0:T(8,128)(2,1)} %get-tuple-element.53), channel_id=1, source_target_pairs={{0,6},{2,0},{4,2},{6,4},{1,7},{3,1},{5,3},{7,5},{8,14},{10,8},{12,... | collective-permute-start | bytes 24584 | tf_op jit(solution)/shard_map/partial_exchange/ppermute | solution.py:802
  19.3 23.7 %copy-start.16 = (f32[32]{0:T(128)S(1)}, f32[32]{0:T(128)}, u32[]{:S(2)}) copy-start(f32[32]{0:T(128)} %constant.171.clone) | copy-start | bytes 388
  19.4 0.6 copy-start.13
  19.4 0.6 copy-start.14
  20.0 0.6 copy-start.15
  33.0 20.3 %all-to-all-start = ((bf16[32,8,1024]{2,1,0:T(8,128)(2,1)}), bf16[32,8,1024]{2,1,0:T(8,128)(2,1)S(1)}, u32[]{:S(2)}, u32[]{:S(2)}) async-start(bf16[32,8,1024]{2,1,0:T(8,128)(2,1)} %bitcast.28), calls=%async_computation | async-start | bytes 1048576 | tf_op jit(solution)/shard_map/dense_exchange/all_to_all | solution.py:854
  38.4 13.7 %collective-permute-start.6 = (bf16[32,128]{1,0:T(8,128)(2,1)}, bf16[32,128]{1,0:T(8,128)(2,1)S(1)}, u32[]{:S(2)}, u32[]{:S(2)}) collective-permute-start(bf16[32,128]{1,0:T(8,128)(2,1)} %get-tuple-element.59), channel_id=1, source_target_pairs={{0,2},{2,4},{4,6},{6,0},{1,3},{3,5},{5,7},{7,1},{8,10},{10,12},{12... | collective-permute-start | bytes 24584 | tf_op jit(solution)/shard_map/latent_exchange/ppermute | solution.py:802
  40.1 11.9 %collective-permute-start.7 = (bf16[32,128]{1,0:T(8,128)(2,1)}, bf16[32,128]{1,0:T(8,128)(2,1)S(1)}, u32[]{:S(2)}, u32[]{:S(2)}) collective-permute-start(bf16[32,128]{1,0:T(8,128)(2,1)} %get-tuple-element.60), channel_id=1, source_target_pairs={{0,4},{2,6},{4,0},{6,2},{1,5},{3,7},{5,1},{7,3},{8,12},{10,14},{12... | collective-permute-start | bytes 24584 | tf_op jit(solution)/shard_map/latent_exchange/ppermute | solution.py:802
  41.6 10.5 %collective-permute-start.8 = (bf16[32,128]{1,0:T(8,128)(2,1)}, bf16[32,128]{1,0:T(8,128)(2,1)S(1)}, u32[]{:S(2)}, u32[]{:S(2)}) collective-permute-start(bf16[32,128]{1,0:T(8,128)(2,1)} %get-tuple-element.61), channel_id=1, source_target_pairs={{0,6},{2,0},{4,2},{6,4},{1,7},{3,1},{5,3},{7,5},{8,14},{10,8},{12,... | collective-permute-start | bytes 24584 | tf_op jit(solution)/shard_map/latent_exchange/ppermute | solution.py:802
  45.0 5.8 %copy-start.12 = (f32[1024]{0:T(1024)S(1)}, f32[1024]{0:T(1024)}, u32[]{:S(2)}) copy-start(f32[1024]{0:T(1024)} %constant.170.clone) | copy-start | bytes 12292
  52.1 12.3 %copy-start.9 = (bf16[32,128]{1,0:T(8,128)(2,1)}, bf16[32,128]{1,0:T(8,128)(2,1)S(1)}, u32[]{:S(2)}) copy-start(bf16[32,128]{1,0:T(8,128)(2,1)S(1)} %collective-permute-done.6.refs_3_) | copy-start | bytes 24580
  52.1 12.3 %copy-start.10 = (bf16[32,128]{1,0:T(8,128)(2,1)}, bf16[32,128]{1,0:T(8,128)(2,1)S(1)}, u32[]{:S(2)}) copy-start(bf16[32,128]{1,0:T(8,128)(2,1)S(1)} %collective-permute-done.7.refs_4_) | copy-start | bytes 24580
  52.1 12.3 %copy-start.11 = (bf16[32,128]{1,0:T(8,128)(2,1)}, bf16[32,128]{1,0:T(8,128)(2,1)S(1)}, u32[]{:S(2)}) copy-start(bf16[32,128]{1,0:T(8,128)(2,1)S(1)} %collective-permute-done.8.refs_5_) | copy-start | bytes 24580
  53.3 0.8 copy-start
  64.3 20.5 %copy-start.7 = (f32[1024]{0:T(1024)S(1)}, f32[1024]{0:T(1024)}, u32[]{:S(2)}) copy-start(f32[1024]{0:T(1024)} %broadcast_multiply_fusion) | copy-start | bytes 12292
  64.4 13.7 %all-to-all-start.1 = ((bf16[32,32,128]{2,1,0:T(8,128)(2,1)}), bf16[32,32,128]{2,1,0:T(8,128)(2,1)S(1)}, u32[]{:S(2)}, u32[]{:S(2)}) async-start(bf16[32,32,128]{2,1,0:T(8,128)(2,1)} %get-tuple-element.63), calls=%async_computation.1 | async-start | bytes 524288 | tf_op jit(solution)/shard_map/preact_exchange/all_to_all | solution.py:907
  69.3 7.0 %collective-permute-start.9 = (f32[32,1024]{1,0:T(8,128)S(1)}, f32[32,1024]{1,0:T(8,128)S(1)}, u32[]{:S(2)}, u32[]{:S(2)}) collective-permute-start(f32[32,1024]{1,0:T(8,128)S(1)} %get-tuple-element.95), channel_id=1, source_target_pairs={{0,1},{1,0},{2,3},{3,2},{4,5},{5,4},{6,7},{7,6},{8,9},{9,8},{10,11... | collective-permute-start | bytes 393224 | tf_op jit(solution)/shard_map/coefficient_swap/ppermute | solution.py:912
  76.3 36.0 %copy-start.6 = (f32[32,1024]{1,0:T(8,128)}, f32[32,1024]{1,0:T(8,128)S(1)}, u32[]{:S(2)}) copy-start(f32[32,1024]{1,0:T(8,128)S(1)} %collective-permute-done.9.coef_ref) | copy-start | bytes 393220
  78.0 0.7 copy-start.2
  80.7 17.3 %all-to-all-start.2 = ((bf16[32,32,128]{2,1,0:T(8,128)(2,1)}), bf16[32,32,128]{2,1,0:T(8,128)(2,1)S(1)}, u32[]{:S(2)}, u32[]{:S(2)}) async-start(bf16[32,32,128]{2,1,0:T(8,128)(2,1)} %get-tuple-element.73), calls=%async_computation.2 | async-start | bytes 524288 | tf_op jit(solution)/shard_map/cell_grads_all/all_to_all | solution.py:928
  98.1 0.7 copy-start.1
  98.8 19.4 %copy-start.8 = (f32[40,64]{1,0:T(8,128)S(1)}, f32[40,64]{1,0:T(8,128)}, u32[]{:S(2)}) copy-start(f32[40,64]{1,0:T(8,128)} %get-tuple-element.88) | copy-start | bytes 30724
  112.3 16.5 %all-to-all-start.3 = ((bf16[32,32,128]{2,1,0:T(8,128)(2,1)}), bf16[32,32,128]{2,1,0:T(8,128)(2,1)S(1)}, u32[]{:S(2)}, u32[]{:S(2)}) async-start(bf16[32,32,128]{2,1,0:T(8,128)(2,1)} %get-tuple-element.82), calls=%async_computation.3 | async-start | bytes 524288 | tf_op jit(solution)/shard_map/latent_grad_exchange/all_to_all | solution.py:966
  125.1 18.2 %copy-start.3 = (f32[64,1024]{1,0:T(8,128)S(1)}, f32[64,1024]{1,0:T(8,128)}, u32[]{:S(2)}) copy-start(f32[64,1024]{1,0:T(8,128)} %get-tuple-element.83.grad_ref) | copy-start | bytes 786436
  128.8 0.7 copy-start.5
  138.0 14.4 %all-to-all-start.4 = ((bf16[16,40,128]{2,1,0:T(8,128)(2,1)}), bf16[16,40,128]{2,1,0:T(8,128)(2,1)S(1)}, u32[]{:S(2)}, u32[]{:S(2)}) async-start(bf16[16,40,128]{2,1,0:T(8,128)(2,1)} %broadcast_in_dim.49), calls=%async_computation.4 | async-start | bytes 327680 | tf_op jit(solution)/shard_map/weight_sums/all_to_all | solution.py:1022
  143.3 1.6 %collective-permute-start.11 = (f32[64,1024]{1,0:T(8,128)S(1)}, f32[64,1024]{1,0:T(8,128)S(1)}, u32[]{:S(2)}, u32[]{:S(2)}) collective-permute-start(f32[64,1024]{1,0:T(8,128)S(1)} %copy-done.3), channel_id=1, source_target_pairs={{0,1},{1,0},{2,3},{3,2},{4,5},{5,4},{6,7},{7,6},{8,9},{9,8},{10,11... | collective-permute-start | bytes 786440 | tf_op jit(solution)/shard_map/grad_swap/ppermute | solution.py:968
  144.9 0.7 copy-start.4
  152.5 1.2 collective-permute-start.10

commit v2 on v1

--- a/solution.py
+++ b/solution.py
@@ -281,7 +281,7 @@
     if keep:
         g, slope, hid, part_ref, w1, group = rest
     else:
-        g, outs, (w1, group) = rest[0], rest[1:-2], rest[-2:]
+        g, slope, outs, (w1, group) = rest[0], rest[1], rest[2:-2], rest[-2:]
     chan, hidden = second.shape
     wide = BRICK * hidden
     cells = slots.slots * BRICK
@@ -300,8 +300,7 @@
         for q in range(BRICK):
             value, gradient = gelu_pair(base + (sign * q) * w1[2])
             values.append(value.astype(BF16))
-            if keep:
-                slope.ref[pl.ds(row + q * hidden, hidden), :] = gradient.astype(BF16)
+            slope.ref[pl.ds(row + q * hidden, hidden), :] = gradient.astype(BF16)
         all_q = jnp.concatenate(values, axis=0)
         total = dot(f, all_q, NT)
         g.ref[pl.ds(pl.multiple_of(s * chan, chan), chan), :] = total.astype(BF16)
@@ -315,30 +314,12 @@
             sums = jnp.concatenate([sums, jnp.zeros((chan, cells - 128), F32)], axis=1)
         return part + pltpu.roll(sums, s * BRICK, 1)
 
-    kept = (g, slope, hid) if keep else (g,)
+    kept = (g, slope, hid) if keep else (g, slope)
     part = loop(slots.slots, step, jnp.zeros((chan, cells), F32), *kept)
     if keep:
         part_ref[...] = part
     else:
         spread_groups(slots.me, part, outs)
-
-
-def slope_kernel(sign, make, s0, s1, s2, s3, x_ref, first, bias, slope, w1):
-    slots = make((s0, s1, s2, s3))
-    columns(first, bias, w1)
-    hidden = first.shape[1]
-    wide = BRICK * hidden
-
-    def step(s, carry):
-        _, e = slot_points(slots, s, x_ref)
-        base = first_base(sign, e, w1)
-        row = pl.multiple_of(s * wide, wide)
-        for q in range(BRICK):
-            _, gradient = gelu_pair(base + (sign * q) * w1[2])
-            slope.ref[pl.ds(row + q * hidden, hidden), :] = gradient.astype(BF16)
-        return carry
-
-    loop(slots.slots, step, 0, slope)
 
 
 def back_kernel(sign, weight, decode, make, s0, s1, s2, s3, x_ref, f_ref, second, *rest):
@@ -348,7 +329,7 @@
         gp = gp_ref[...]
         dec[...] = jnp.zeros_like(dec)
     else:
-        own_ref, recv_ref, g, slope, out_ref = rest
+        own_ref, recv_ref, other_ref, g, slope, out_ref = rest
         gp = own_ref[...] + jnp.sum(recv_ref[...].astype(F32), axis=0)
     chan, hidden = second.shape
     wide = BRICK * hidden
@@ -399,9 +380,18 @@
     )
     sums = [jnp.sum(a, axis=1, keepdims=True) for a in acc]
     packed = jnp.concatenate(sums + [jnp.zeros((hidden, 124), F32)], axis=1)
-    out_ref[0:chan, :] = grad2[:, 0:hidden] + grad2[:, hidden : 2 * hidden]
-    out_ref[chan : chan + 8, :] = jnp.transpose(packed)[0:8, :]
+    second_grad = grad2[:, 0:hidden] + grad2[:, hidden : 2 * hidden]
+    grads = jnp.concatenate([second_grad, jnp.transpose(packed)[0:16, :]], axis=0)
+    if not decode:
+        message = jnp.concatenate([grads, other_ref[...]], axis=1).astype(BF16)
+
+        def copy(i, carry):
+            out_ref[i] = message
+            return carry
+
+        lax.fori_loop(0, out_ref.shape[0], copy, 0)
     if decode:
+        out_ref[...] = grads
         for b in range(dec.shape[0]):
             dec_ref[:, b * BLOCK : (b + 1) * BLOCK] = dec[b].astype(BF16)
 
@@ -817,9 +807,9 @@
         return [(a, whole) for a in arrays]
 
     def net(sign, weight, keep, f, layers):
-        outs = [(shape((slots * chan, wide), BF16), by_slot)]
+        outs = [(shape((slots * chan, wide), BF16), by_slot), (hidden_shape, by_slot)]
         if keep:
-            outs += [(hidden_shape, by_slot)] * 2 + [(shape((chan, cells)), whole)]
+            outs += [(hidden_shape, by_slot), (shape((chan, cells)), whole)]
         else:
             outs += [(values_shape, whole)] * subs
         return call(
@@ -828,7 +818,7 @@
         )
 
     with jax.named_scope("encoder_points"):
-        enc_g, *message = net(1.0, QUADRATURE, False, features_t, enc_layers)
+        enc_g, enc_slope, *message = net(1.0, QUADRATURE, False, features_t, enc_layers)
     with jax.named_scope("partial_exchange"):
         partials = ring(message, "sub", subs)
 
@@ -928,9 +918,10 @@
         all_grads = lax.all_to_all(cell_grads, every, 0, 0, tiled=True)
 
     def back(sign, weight, decode, f, layers, operands, saved):
-        outs = [(shape((chan + 8, hidden)), whole)]
+        outs = [(shape((devices, chan + 16, 2 * hidden), BF16), whole)]
         scratch = []
         if decode:
+            outs = [(shape((chan + 16, hidden)), whole)]
             outs.append((shape((chan, points), BF16), whole))
             scratch.append(pltpu.VMEM((blocks_here, chan, BLOCK), F32))
         return call(
@@ -946,15 +937,8 @@
             [dec_g, dec_slope, dec_hid],
         )
 
-    with jax.named_scope("encoder_slope"):
-        slope_coords, _ = hold(coords, cell_grads)
-        (enc_slope,) = call(
-            functools.partial(slope_kernel, 1.0, make),
-            [*scal, *wholes(slope_coords, *enc_layers[0:2])],
-            [(hidden_shape, by_slot)], [w1_scratch], 1e9, 4e6,
-        )
     with jax.named_scope("mix_back"):
-        all_grads, decoded, enc_slope = hold(all_grads, decoded, enc_slope)
+        all_grads, decoded = hold(all_grads, decoded)
         sent_back, grad_modes = call(
             mixback_kernel,
             [(core, "scalar"), *wholes(all_grads, scale_column, scale_row), (spectral, "raw"),
@@ -1009,19 +993,17 @@
     with jax.named_scope("encoder_back"):
         arrived_back, own_grads, grad_spectral = hold(arrived_back, own_grads, grad_spectral)
         (enc_grads,) = back(
-            1.0, QUADRATURE, False, features_t, enc_layers, [own_grads, arrived_back],
+            1.0, QUADRATURE, False, features_t, enc_layers, [own_grads, arrived_back, dec_grads],
             [enc_g, enc_slope],
         )
     with jax.named_scope("grad_spectral_far"):
         grad_far, _ = hold(grad_far, enc_grads)
         grad_spectral = outer(1 - core, coef_far, grad_far, grad_spectral)
     with jax.named_scope("weight_sums"):
-        both = jnp.concatenate([enc_grads, dec_grads], axis=1).astype(BF16)
-        spread = jnp.broadcast_to(both[None], (devices,) + both.shape)
         total = jnp.sum(
-            lax.all_to_all(spread, ("slab", "sub"), 0, 0, tiled=True).astype(F32), axis=0
-        )
-        small = total[chan:]
+            lax.all_to_all(enc_grads, ("slab", "sub"), 0, 0, tiled=True).astype(F32), axis=0
+        )
+        small = total[chan : chan + 8]
         small = small + lax.ppermute(small, "chan", swap)
     enc_second = total[:chan, :hidden].T
     dec_second = total[:chan, hidden:].T

time: 156 us -> 151 us (0.968)
  Pallas kernels: 91.6 us -> 88.2 us
  starting transfers between devices: 38.9 us -> 36.8 us
  waiting for transfers between devices: 6.84 us -> 8.93 us
    pallas_call x11 -> x10, Pallas kernels: 78 us -> 74.6 us  [call(): pl.pallas_call(wrapped, out_shape=[jax.ShapeDtypeStruct(o.shape, o.dtype)...]
    all_to_all x1, starting transfers between devices: 5.85 us -> 3.74 us  [body(): arrived_back = lax.all_to_all(sent_back, every, 0, 0, tiled=True)]
    all_to_all x1, waiting for transfers between devices: 0.01 us -> 2.1 us  [body(): all_grads = lax.all_to_all(cell_grads, every, 0, 0, tiled=True)]
    unnamed x34 -> x32, local copies, waits for them, and re-layouts: 4.39 us -> 4.43 us
  transfers between devices with their start and end apart: 17 -> 17, of which waited for: 6 -> 7; matrix products, arithmetic and copies ran while one was open for 6% -> 6% of each run, Pallas kernels for 26% -> 24%
where the time goes in v2:
time: 151 us; the launch traced here: 150 us
  Pallas kernels  88.2 us (58%)
  starting transfers between devices  36.8 us (24%)
  local copies, waits for them, and re-layouts  12.2 us (8%)
  waiting for transfers between devices  8.93 us (6%)
  other arithmetic  2.84 us (2%)
    pallas_call x10, Pallas kernels, call(): pl.pallas_call(wrapped, out_shape=[jax.ShapeDtypeStruct(o.shape, o.dtype)...  74.6 us
    ppermute x9, starting transfers between devices, ring(): lax.ppermute(values[k], axis, [(i, (i + k) % size) for i in range(size)])  15.3 us
    pallas_call x2, Pallas kernels, outer(): pl.pallas_call(outer_kernel, grid_spec=pltpu.PrefetchScalarGridSpec(num_s...  13.7 us
    all_to_all x1, starting transfers between devices, body(): lax.all_to_all(enc_grads, ('slab', 'sub'), 0, 0, tiled=True).astype(F32)  5.26 us
    all_to_all x1, starting transfers between devices, body(): dense = lax.all_to_all(dense, every, 0, 0, tiled=True)  4.81 us
    unnamed x32, local copies, waits for them, and re-layouts  4.43 us
    all_to_all x1, starting transfers between devices, body(): all_grads = lax.all_to_all(cell_grads, every, 0, 0, tiled=True)  4.11 us
    all_to_all x1, starting transfers between devices, body(): arrived_back = lax.all_to_all(sent_back, every, 0, 0, tiled=True)  3.74 us
  transfers between devices with their start and end apart: 17, of which 7 were waited for; matrix products, arithmetic and copies ran while one was open for 6% of the time, Pallas kernels for 24%

profile of v2, /device:TPU:0, one launch (start us, length us, event | category | flops | bytes accessed | tf_op | source)
XLA Modules:
  0.0 150.1 jit_solution(18032611971940245339)
XLA Ops:
  0.6 6.9 %encoder_points.1 = (bf16[512,512]{1,0:T(8,128)(2,1)}, bf16[8192,128]{1,0:T(8,128)(2,1)}, bf16[32,128]{1,0:T(8,128)(2,1)}, bf16[32,128]{1,0:T(8,128)(2,1)}, bf16...) custom-call(s32[1,4,4,4]{3,2,1,0:T(4,128)} %refs_0_.11, s32[1,4,4,4]{3,2,1,0:T(4,128)} %refs_1_.12, s32[1,4,4]{2,1,0:T(4,128)} %refs_2_.13, ...), custom_call_target="tpu_custom_call" | custom-call | flops 1000000000 | bytes 8000000 | tf_op jit(solution)/shard_map/encoder_points/pallas_call | solution.py:150
  7.6 5.1 %collective-permute-start.5 = (s32[4,4,4]{2,1,0:T(4,128)}, s32[4,4,4]{2,1,0:T(4,128)S(1)}, u32[]{:S(2)}, u32[]{:S(2)}) collective-permute-start(s32[4,4,4]{2,1,0:T(4,128)} %bitcast.34), channel_id=1, source_target_pairs={{0,24},{8,0},{16,8},{24,16},{1,25},{9,1},{17,9},{25,17},{2,26},{10... | collective-permute-start | bytes 776 | tf_op jit(solution)/shard_map/slots_all/ppermute | solution.py:792
  12.7 1.0 collective-permute-start.3
  13.7 1.5 collective-permute-start
  15.2 1.5 %collective-permute-start.1 = (bf16[32,128]{1,0:T(8,128)(2,1)}, bf16[32,128]{1,0:T(8,128)(2,1)S(1)}, u32[]{:S(2)}, u32[]{:S(2)}) collective-permute-start(bf16[32,128]{1,0:T(8,128)(2,1)} %get-tuple-element.51), channel_id=1, source_target_pairs={{0,4},{2,6},{4,0},{6,2},{1,5},{3,7},{5,1},{7,3},{8,12},{10,14},{12... | collective-permute-start | bytes 24584 | tf_op jit(solution)/shard_map/partial_exchange/ppermute | solution.py:792
  17.1 1.5 collective-permute-start.2
  18.5 0.7 pad_add_fusion
  19.3 0.6 gather_fusion
  21.1 0.6 copy-done.14
  21.7 12.4 %dense_transform.1 = (bf16[256,1024]{1,0:T(8,128)(2,1)}, bf16[32,128]{1,0:T(8,128)(2,1)}, bf16[32,128]{1,0:T(8,128)(2,1)}, bf16[32,128]{1,0:T(8,128)(2,1)}, bf16[32,128]{1,0:T(8,128)(2,1)}) custom-call(s32[1,4,4,4]{3,2,1,0:T(4,128)} %refs_0_.11, s32[1,4,4,4]{3,2,1,0:T(4,128)} %refs_1_.12, s32[1,4,4]{2,1,0:T(4,128)} %refs_2_.13, s32[8]{0:T(128)} %refs_3_.11, ...), custom_call_target="tpu_custom_call" | custom-call | flops 8000000000 | bytes 10000000 | tf_op jit(solution)/shard_map/dense_transform/pallas_call | solution.py:150
  34.1 4.8 %all-to-all-start = ((bf16[32,8,1024]{2,1,0:T(8,128)(2,1)}), bf16[32,8,1024]{2,1,0:T(8,128)(2,1)S(1)}, u32[]{:S(2)}, u32[]{:S(2)}) async-start(bf16[32,8,1024]{2,1,0:T(8,128)(2,1)} %bitcast.28), calls=%async_computation | async-start | bytes 1048576 | tf_op jit(solution)/shard_map/dense_exchange/all_to_all | solution.py:844
  38.9 0.6 add_convert_fusion.refs_0_.refs_4_
  39.5 1.8 %collective-permute-start.6 = (bf16[32,128]{1,0:T(8,128)(2,1)}, bf16[32,128]{1,0:T(8,128)(2,1)S(1)}, u32[]{:S(2)}, u32[]{:S(2)}) collective-permute-start(bf16[32,128]{1,0:T(8,128)(2,1)} %get-tuple-element.58), channel_id=1, source_target_pairs={{0,2},{2,4},{4,6},{6,0},{1,3},{3,5},{5,7},{7,1},{8,10},{10,12},{12... | collective-permute-start | bytes 24584 | tf_op jit(solution)/shard_map/latent_exchange/ppermute | solution.py:792
  41.3 1.5 collective-permute-start.7
  42.8 1.5 collective-permute-start.8
  44.2 0.6 dynamic_slice.13
  44.8 0.7 dynamic-slice_reduce_fusion
  45.5 0.6 broadcast_in_dim.40.refs_3_
  46.1 5.8 %cell_basis.1.refs_5_ = bf16[1024,2048]{1,0:T(8,128)(2,1)} custom-call(f32[3,2048]{1,0:T(4,128)} %add_convert_fusion.refs_0_.refs_4_, bf16[1024,256]{1,0:T(8,128)(2,1)} %constant.166.clone.refs_1_, bf16[1024,256]{1,0:T(8,128)(2,1)} %constant.167.clone.refs_2_, bf16[16,256]{1,0:T(8,128)(2,1)} %broadcast_in_dim.40.refs_3_), custom_call_target="tpu_custom_call" | custom-call | flops 5000000000 | bytes 8000000 | tf_op jit(solution)/shard_map/cell_basis/pallas_call | solution.py:150
  52.0 1.2 broadcast_multiply_fusion
  53.3 1.2 all-to-all-done
  54.5 0.8 copy-done
  55.3 10.2 %mix.1 = (bf16[32,32,128]{2,1,0:T(8,128)(2,1)}, f32[64,1024]{1,0:T(8,128)}) custom-call(s32[1]{0:T(128)} %bitcast.refs_0_.place, bf16[16,2,8,1024]{3,2,1,0:T(8,128)(2,1)} %bitcast.27, bf16[64,128]{1,0:T(8,128)(2,1)} %constant.163.clone.refs_2_, f32[1,1024]{1,0:T(1,128)} %bitcast.31, bf16[64,32,64,64]{3,2,1,0:T(8,128)(2,1)} %refs_4_.11, ...), custom_call_target="tpu_custom_call" | custom-call | flops 4000000000 | bytes 20000000 | tf_op jit(solution)/shard_map/mix/pallas_call | solution.py:150
  65.5 3.3 %all-to-all-start.1 = ((bf16[32,32,128]{2,1,0:T(8,128)(2,1)}), bf16[32,32,128]{2,1,0:T(8,128)(2,1)S(1)}, u32[]{:S(2)}, u32[]{:S(2)}) async-start(bf16[32,32,128]{2,1,0:T(8,128)(2,1)} %get-tuple-element.62), calls=%async_computation.1 | async-start | bytes 524288 | tf_op jit(solution)/shard_map/preact_exchange/all_to_all | solution.py:897
  68.8 1.6 %constant_dynamic-slice_fusion = (f32[32,1024]{1,0:T(8,128)}, f32[32,1024]{1,0:T(8,128)S(1)}) fusion(f32[64,1024]{1,0:T(8,128)} %get-tuple-element.65, s32[]{:T(128)S(6)} %select_n.146, s32[]{:T(128)S(6)} %select_n.145), kind=kLoop, calls=%fused_computation.36 | loop fusion | bytes 524296 | tf_op jit(solution)/shard_map/coefficient_swap/dynamic_slice | solution.py:900
  70.5 7.0 %decoder_points.1 = (bf16[512,512]{1,0:T(8,128)(2,1)}, bf16[8192,128]{1,0:T(8,128)(2,1)}, bf16[8192,128]{1,0:T(8,128)(2,1)}, f32[32,128]{1,0:T(8,128)}) custom-call(s32[1,4,4,4]{3,2,1,0:T(4,128)} %refs_0_.11, s32[1,4,4,4]{3,2,1,0:T(4,128)} %refs_1_.12, s32[1,4,4]{2,1,0:T(4,128)} %refs_2_.13, s32[8]{0:T(128)} %refs_3_.11, f32[3,1024]{1,0:T(4,128)} %refs_4_.12, ...), custom_call_target="tpu_custom_call" | custom-call | flops 1000000000 | bytes 8000000 | tf_op jit(solution)/shard_map/decoder_points/pallas_call | solution.py:150
  77.5 1.7 %all-to-all-done.1.refs_0_ = bf16[32,32,128]{2,1,0:T(8,128)(2,1)S(1)} async-done(((bf16[32,32,128]{2,1,0:T(8,128)(2,1)}), bf16[32,32,128]{2,1,0:T(8,128)(2,1)S(1)}, u32[]{:S(2)}, u32[]{:S(2)}) %all-to-all-start.1) | async-done | bytes 262176 | tf_op jit(solution)/shard_map/preact_exchange/all_to_all | solution.py:897
  79.2 0.7 copy-done.2
  80.0 2.0 %cell_values.1 = (bf16[32,32,128]{2,1,0:T(8,128)(2,1)}, f32[32,128]{1,0:T(8,128)}) custom-call(bf16[32,32,128]{2,1,0:T(8,128)(2,1)} %copy-done.2, f32[32,128]{1,0:T(8,128)} %get-tuple-element.67.refs_1_, bf16[32,128]{1,0:T(8,128)(2,1)} %get-tuple-element.68.refs_2_, bf16[32,128]{1,0:T(8,128)(2,1)} %copy-done.8, bf16[32,128]{1,0:T(8,128)(2,1)} %copy-done.9, ...), custom_call_target="tpu_custom_call" | custom-call | flops 1000000 | bytes 1000000 | tf_op jit(solution)/shard_map/cell_values/pallas_call | solution.py:150
  82.0 4.1 %all-to-all-start.2 = ((bf16[32,32,128]{2,1,0:T(8,128)(2,1)}), bf16[32,32,128]{2,1,0:T(8,128)(2,1)S(1)}, u32[]{:S(2)}, u32[]{:S(2)}) async-start(bf16[32,32,128]{2,1,0:T(8,128)(2,1)} %get-tuple-element.72), calls=%async_computation.2 | async-start | bytes 524288 | tf_op jit(solution)/shard_map/cell_grads_all/all_to_all | solution.py:918
  86.1 1.1 copy.36.refs_2_
  87.2 7.4 %decoder_back.1 = (f32[48,64]{1,0:T(8,128)}, bf16[32,1024]{1,0:T(8,128)(2,1)}) custom-call(s32[1,4,4,4]{3,2,1,0:T(4,128)} %refs_0_.11, s32[1,4,4,4]{3,2,1,0:T(4,128)} %refs_1_.12, s32[1,4,4]{2,1,0:T(4,128)} %refs_2_.13, s32[8]{0:T(128)} %refs_3_.11, f32[3,1024]{1,0:T(4,128)} %refs_4_.12, bf16[32,1024]{1,0:T(8,128)(2,1)} %bitcast.30, f32[32,64]{1,0:T(8,128)} %bitcast.38, ...), custom_call_target="tpu_custom_call" | custom-call | flops 1000000000 | bytes 8000000 | tf_op jit(solution)/shard_map/decoder_back/pallas_call | solution.py:150
  94.6 2.1 %all-to-all-done.2.refs_1_.refs_5_ = bf16[32,32,128]{2,1,0:T(8,128)(2,1)S(1)} async-done(((bf16[32,32,128]{2,1,0:T(8,128)(2,1)}), bf16[32,32,128]{2,1,0:T(8,128)(2,1)S(1)}, u32[]{:S(2)}, u32[]{:S(2)}) %all-to-all-start.2) | async-done | bytes 262176 | tf_op jit(solution)/shard_map/cell_grads_all/all_to_all | solution.py:918
  96.7 0.7 copy-done.1
  97.4 13.5 %mix_back.1 = (bf16[32,32,128]{2,1,0:T(8,128)(2,1)}, f32[64,1024]{1,0:T(8,128)}) custom-call(s32[1]{0:T(128)} %bitcast.refs_0_.place, bf16[32,32,128]{2,1,0:T(8,128)(2,1)} %copy-done.1, f32[1024,1]{1,0:T(8,128)} %copy.36.refs_2_, f32[1,1024]{1,0:T(1,128)} %bitcast.32, bf16[64,32,64,64]{3,2,1,0:T(8,128)(2,1)} %refs_4_.11, bf16[1024,2048]{1,0:T(8,128)(2,1)} %cell_basis.1.refs_5_), custom_call_target="tpu_custom_call" | custom-call | flops 4000000000 | bytes 20000000 | tf_op jit(solution)/shard_map/mix_back/pallas_call | solution.py:150
  110.9 3.7 %all-to-all-start.3 = ((bf16[32,32,128]{2,1,0:T(8,128)(2,1)}), bf16[32,32,128]{2,1,0:T(8,128)(2,1)S(1)}, u32[]{:S(2)}, u32[]{:S(2)}) async-start(bf16[32,32,128]{2,1,0:T(8,128)(2,1)} %get-tuple-element.80), calls=%async_computation.3 | async-start | bytes 524288 | tf_op jit(solution)/shard_map/latent_grad_exchange/all_to_all | solution.py:950
  114.7 6.8 %grad_spectral.1.rest_0_ = bf16[64,32,32,64]{3,2,1,0:T(8,128)(2,1)} custom-call(s32[1]{0:T(128)} %bitcast.refs_0_.place, f32[32,1024]{1,0:T(8,128)} %get-tuple-element.92.coef_ref, f32[64,1024]{1,0:T(8,128)} %get-tuple-element.81.grad_ref), custom_call_target="tpu_custom_call" | custom-call | flops 10000000 | bytes 10000000 | tf_op jit(solution)/shard_map/grad_spectral/pallas_call | solution.py:970
  121.5 2.1 %own_cells.1.refs_7_ = f32[32,128]{1,0:T(8,128)} custom-call(s32[1,4,4,4]{3,2,1,0:T(4,128)} %refs_0_.11, s32[1,4,4,4]{3,2,1,0:T(4,128)} %refs_1_.12, s32[1,4,4]{2,1,0:T(4,128)} %refs_2_.13, s32[8]{0:T(128)} %refs_3_.11, f32[3,2048]{1,0:T(4,128)} %add_convert_fusion.refs_0_.refs_4_, bf16[32,32,128]{2,1,0:T(8,128)(2,1)} %copy-done.1), custom_call_target="tpu_custom_call" | custom-call | flops 100000000 | bytes 1000000 | tf_op jit(solution)/shard_map/own_cells/pallas_call | solution.py:150
  123.7 1.6 %all-to-all-done.3.refs_8_ = bf16[32,32,128]{2,1,0:T(8,128)(2,1)S(1)} async-done(((bf16[32,32,128]{2,1,0:T(8,128)(2,1)}), bf16[32,32,128]{2,1,0:T(8,128)(2,1)S(1)}, u32[]{:S(2)}, u32[]{:S(2)}) %all-to-all-start.3) | async-done | bytes 262176 | tf_op jit(solution)/shard_map/latent_grad_exchange/all_to_all | solution.py:950
  125.3 0.7 copy-done.5
  126.0 7.2 %encoder_back.1 = bf16[16,48,128]{2,1,0:T(8,128)(2,1)} custom-call(s32[1,4,4,4]{3,2,1,0:T(4,128)} %refs_0_.11, s32[1,4,4,4]{3,2,1,0:T(4,128)} %refs_1_.12, s32[1,4,4]{2,1,0:T(4,128)} %refs_2_.13, s32[8]{0:T(128)} %refs_3_.11, f32[3,1024]{1,0:T(4,128)} %refs_4_.12, bf16[32,1024]{1,0:T(8,128)(2,1)} %bitcast.43, f32[32,64]{1,0:T(8,128)} %bitcast.46, ...), custom_call_target="tpu_custom_call" | custom-call | flops 1000000000 | bytes 8000000 | tf_op jit(solution)/shard_map/encoder_back/pallas_call | solution.py:150
  133.2 5.3 %all-to-all-start.4 = ((bf16[16,48,128]{2,1,0:T(8,128)(2,1)}), bf16[16,48,128]{2,1,0:T(8,128)(2,1)S(1)}, u32[]{:S(2)}, u32[]{:S(2)}) async-start(bf16[16,48,128]{2,1,0:T(8,128)(2,1)} %encoder_back.1), calls=%async_computation.4 | async-start | bytes 393216 | tf_op jit(solution)/shard_map/weight_sums/all_to_all | solution.py:1004
  138.5 1.5 %collective-permute-done.11.grad_ref = f32[64,1024]{1,0:T(8,128)S(1)} collective-permute-done((f32[64,1024]{1,0:T(8,128)S(1)}, f32[64,1024]{1,0:T(8,128)S(1)}, u32[]{:S(2)}, u32[]{:S(2)}) %collective-permute-start.11) | collective-permute-done | bytes 262176 | tf_op jit(solution)/shard_map/grad_swap/ppermute | solution.py:952
  140.1 0.7 copy-done.4
  140.7 6.8 %grad_spectral_far.1 = bf16[64,32,32,64]{3,2,1,0:T(8,128)(2,1)} custom-call(s32[1]{0:T(128)S(6)} %sub.47.place, f32[32,1024]{1,0:T(8,128)} %copy-done.6, f32[64,1024]{1,0:T(8,128)} %copy-done.4, bf16[64,32,32,64]{3,2,1,0:T(8,128)(2,1)} %grad_spectral.1.rest_0_), custom_call_target="tpu_custom_call", output_to_operand_aliasing={{}: (3, {})} | custom-call | flops 10000000 | bytes 10000000 | tf_op jit(solution)/shard_map/grad_spectral_far/pallas_call | solution.py:970
  147.8 0.7 slice_bitcast_fusion
  148.9 0.7 fusion.6
  149.5 0.6 slice_bitcast_fusion.2
  (60 shorter events, 2.3 us)
Async XLA Ops:
  7.6 9.5 %collective-permute-start.5 = (s32[4,4,4]{2,1,0:T(4,128)}, s32[4,4,4]{2,1,0:T(4,128)S(1)}, u32[]{:S(2)}, u32[]{:S(2)}) collective-permute-start(s32[4,4,4]{2,1,0:T(4,128)} %bitcast.34), channel_id=1, source_target_pairs={{0,24},{8,0},{16,8},{24,16},{1,25},{9,1},{17,9},{25,17},{2,26},{10... | collective-permute-start | bytes 776 | tf_op jit(solution)/shard_map/slots_all/ppermute | solution.py:792
  12.7 5.9 %collective-permute-start.4 = (s32[4,4,4]{2,1,0:T(4,128)}, s32[4,4,4]{2,1,0:T(4,128)S(1)}, u32[]{:S(2)}, u32[]{:S(2)}) collective-permute-start(s32[4,4,4]{2,1,0:T(4,128)} %bitcast.35), channel_id=1, source_target_pairs={{0,16},{8,24},{16,0},{24,8},{1,17},{9,25},{17,1},{25,9},{2,18},{10... | collective-permute-start | bytes 776 | tf_op jit(solution)/shard_map/slots_all/ppermute | solution.py:792
  12.7 5.9 %collective-permute-start.3 = (s32[4,4,4]{2,1,0:T(4,128)}, s32[4,4,4]{2,1,0:T(4,128)S(1)}, u32[]{:S(2)}, u32[]{:S(2)}) collective-permute-start(s32[4,4,4]{2,1,0:T(4,128)} %bitcast.36), channel_id=1, source_target_pairs={{0,8},{8,16},{16,24},{24,0},{1,9},{9,17},{17,25},{25,1},{2,10},{10... | collective-permute-start | bytes 776 | tf_op jit(solution)/shard_map/slots_all/ppermute | solution.py:792
  13.7 6.8 %collective-permute-start = (bf16[32,128]{1,0:T(8,128)(2,1)}, bf16[32,128]{1,0:T(8,128)(2,1)S(1)}, u32[]{:S(2)}, u32[]{:S(2)}) collective-permute-start(bf16[32,128]{1,0:T(8,128)(2,1)} %get-tuple-element.50), channel_id=1, source_target_pairs={{0,2},{2,4},{4,6},{6,0},{1,3},{3,5},{5,7},{7,1},{8,10},{10,12},{12... | collective-permute-start | bytes 24584 | tf_op jit(solution)/shard_map/partial_exchange/ppermute | solution.py:792
  15.2 5.3 %collective-permute-start.1 = (bf16[32,128]{1,0:T(8,128)(2,1)}, bf16[32,128]{1,0:T(8,128)(2,1)S(1)}, u32[]{:S(2)}, u32[]{:S(2)}) collective-permute-start(bf16[32,128]{1,0:T(8,128)(2,1)} %get-tuple-element.51), channel_id=1, source_target_pairs={{0,4},{2,6},{4,0},{6,2},{1,5},{3,7},{5,1},{7,3},{8,12},{10,14},{12... | collective-permute-start | bytes 24584 | tf_op jit(solution)/shard_map/partial_exchange/ppermute | solution.py:792
  17.1 3.9 %collective-permute-start.2 = (bf16[32,128]{1,0:T(8,128)(2,1)}, bf16[32,128]{1,0:T(8,128)(2,1)S(1)}, u32[]{:S(2)}, u32[]{:S(2)}) collective-permute-start(bf16[32,128]{1,0:T(8,128)(2,1)} %get-tuple-element.52), channel_id=1, source_target_pairs={{0,6},{2,0},{4,2},{6,4},{1,7},{3,1},{5,3},{7,5},{8,14},{10,8},{12,... | collective-permute-start | bytes 24584 | tf_op jit(solution)/shard_map/partial_exchange/ppermute | solution.py:792
  20.5 23.8 %copy-start.15 = (f32[32]{0:T(128)S(1)}, f32[32]{0:T(128)}, u32[]{:S(2)}) copy-start(f32[32]{0:T(128)} %constant.171.clone) | copy-start | bytes 388
  20.5 0.6 copy-start.12
  20.5 0.6 copy-start.13
  21.1 0.6 copy-start.14
  34.1 20.4 %all-to-all-start = ((bf16[32,8,1024]{2,1,0:T(8,128)(2,1)}), bf16[32,8,1024]{2,1,0:T(8,128)(2,1)S(1)}, u32[]{:S(2)}, u32[]{:S(2)}) async-start(bf16[32,8,1024]{2,1,0:T(8,128)(2,1)} %bitcast.28), calls=%async_computation | async-start | bytes 1048576 | tf_op jit(solution)/shard_map/dense_exchange/all_to_all | solution.py:844
  39.5 13.7 %collective-permute-start.6 = (bf16[32,128]{1,0:T(8,128)(2,1)}, bf16[32,128]{1,0:T(8,128)(2,1)S(1)}, u32[]{:S(2)}, u32[]{:S(2)}) collective-permute-start(bf16[32,128]{1,0:T(8,128)(2,1)} %get-tuple-element.58), channel_id=1, source_target_pairs={{0,2},{2,4},{4,6},{6,0},{1,3},{3,5},{5,7},{7,1},{8,10},{10,12},{12... | collective-permute-start | bytes 24584 | tf_op jit(solution)/shard_map/latent_exchange/ppermute | solution.py:792
  41.3 11.9 %collective-permute-start.7 = (bf16[32,128]{1,0:T(8,128)(2,1)}, bf16[32,128]{1,0:T(8,128)(2,1)S(1)}, u32[]{:S(2)}, u32[]{:S(2)}) collective-permute-start(bf16[32,128]{1,0:T(8,128)(2,1)} %get-tuple-element.59), channel_id=1, source_target_pairs={{0,4},{2,6},{4,0},{6,2},{1,5},{3,7},{5,1},{7,3},{8,12},{10,14},{12... | collective-permute-start | bytes 24584 | tf_op jit(solution)/shard_map/latent_exchange/ppermute | solution.py:792
  42.8 10.5 %collective-permute-start.8 = (bf16[32,128]{1,0:T(8,128)(2,1)}, bf16[32,128]{1,0:T(8,128)(2,1)S(1)}, u32[]{:S(2)}, u32[]{:S(2)}) collective-permute-start(bf16[32,128]{1,0:T(8,128)(2,1)} %get-tuple-element.60), channel_id=1, source_target_pairs={{0,6},{2,0},{4,2},{6,4},{1,7},{3,1},{5,3},{7,5},{8,14},{10,8},{12,... | collective-permute-start | bytes 24584 | tf_op jit(solution)/shard_map/latent_exchange/ppermute | solution.py:792
  46.1 5.8 %copy-start.11 = (f32[1024]{0:T(1024)S(1)}, f32[1024]{0:T(1024)}, u32[]{:S(2)}) copy-start(f32[1024]{0:T(1024)} %constant.170.clone) | copy-start | bytes 12292
  53.2 12.3 %copy-start.8 = (bf16[32,128]{1,0:T(8,128)(2,1)}, bf16[32,128]{1,0:T(8,128)(2,1)S(1)}, u32[]{:S(2)}) copy-start(bf16[32,128]{1,0:T(8,128)(2,1)S(1)} %collective-permute-done.6.refs_3_) | copy-start | bytes 24580
  53.2 12.3 %copy-start.9 = (bf16[32,128]{1,0:T(8,128)(2,1)}, bf16[32,128]{1,0:T(8,128)(2,1)S(1)}, u32[]{:S(2)}) copy-start(bf16[32,128]{1,0:T(8,128)(2,1)S(1)} %collective-permute-done.7.refs_4_) | copy-start | bytes 24580
  53.3 12.3 %copy-start.10 = (bf16[32,128]{1,0:T(8,128)(2,1)}, bf16[32,128]{1,0:T(8,128)(2,1)S(1)}, u32[]{:S(2)}) copy-start(bf16[32,128]{1,0:T(8,128)(2,1)S(1)} %collective-permute-done.8.refs_5_) | copy-start | bytes 24580
  54.5 0.8 copy-start
  65.5 20.6 %copy-start.7 = (f32[1024]{0:T(1024)S(1)}, f32[1024]{0:T(1024)}, u32[]{:S(2)}) copy-start(f32[1024]{0:T(1024)} %broadcast_multiply_fusion) | copy-start | bytes 12292
  65.5 13.7 %all-to-all-start.1 = ((bf16[32,32,128]{2,1,0:T(8,128)(2,1)}), bf16[32,32,128]{2,1,0:T(8,128)(2,1)S(1)}, u32[]{:S(2)}, u32[]{:S(2)}) async-start(bf16[32,32,128]{2,1,0:T(8,128)(2,1)} %get-tuple-element.62), calls=%async_computation.1 | async-start | bytes 524288 | tf_op jit(solution)/shard_map/preact_exchange/all_to_all | solution.py:897
  70.5 7.1 %collective-permute-start.9 = (f32[32,1024]{1,0:T(8,128)S(1)}, f32[32,1024]{1,0:T(8,128)S(1)}, u32[]{:S(2)}, u32[]{:S(2)}) collective-permute-start(f32[32,1024]{1,0:T(8,128)S(1)} %get-tuple-element.93), channel_id=1, source_target_pairs={{0,1},{1,0},{2,3},{3,2},{4,5},{5,4},{6,7},{7,6},{8,9},{9,8},{10,11... | collective-permute-start | bytes 393224 | tf_op jit(solution)/shard_map/coefficient_swap/ppermute | solution.py:902
  77.5 33.4 %copy-start.6 = (f32[32,1024]{1,0:T(8,128)}, f32[32,1024]{1,0:T(8,128)S(1)}, u32[]{:S(2)}) copy-start(f32[32,1024]{1,0:T(8,128)S(1)} %collective-permute-done.9.coef_ref) | copy-start | bytes 393220
  79.2 0.7 copy-start.2
  82.0 14.7 %all-to-all-start.2 = ((bf16[32,32,128]{2,1,0:T(8,128)(2,1)}), bf16[32,32,128]{2,1,0:T(8,128)(2,1)S(1)}, u32[]{:S(2)}, u32[]{:S(2)}) async-start(bf16[32,32,128]{2,1,0:T(8,128)(2,1)} %get-tuple-element.72), calls=%async_computation.2 | async-start | bytes 524288 | tf_op jit(solution)/shard_map/cell_grads_all/all_to_all | solution.py:918
  96.7 0.7 copy-start.1
  110.9 14.3 %all-to-all-start.3 = ((bf16[32,32,128]{2,1,0:T(8,128)(2,1)}), bf16[32,32,128]{2,1,0:T(8,128)(2,1)S(1)}, u32[]{:S(2)}, u32[]{:S(2)}) async-start(bf16[32,32,128]{2,1,0:T(8,128)(2,1)} %get-tuple-element.80), calls=%async_computation.3 | async-start | bytes 524288 | tf_op jit(solution)/shard_map/latent_grad_exchange/all_to_all | solution.py:950
  121.5 16.9 %copy-start.3 = (f32[64,1024]{1,0:T(8,128)S(1)}, f32[64,1024]{1,0:T(8,128)}, u32[]{:S(2)}) copy-start(f32[64,1024]{1,0:T(8,128)} %get-tuple-element.81.grad_ref) | copy-start | bytes 786436
  125.3 0.7 copy-start.5
  133.2 14.4 %all-to-all-start.4 = ((bf16[16,48,128]{2,1,0:T(8,128)(2,1)}), bf16[16,48,128]{2,1,0:T(8,128)(2,1)S(1)}, u32[]{:S(2)}, u32[]{:S(2)}) async-start(bf16[16,48,128]{2,1,0:T(8,128)(2,1)} %encoder_back.1), calls=%async_computation.4 | async-start | bytes 393216 | tf_op jit(solution)/shard_map/weight_sums/all_to_all | solution.py:1004
  138.5 1.6 %collective-permute-start.11 = (f32[64,1024]{1,0:T(8,128)S(1)}, f32[64,1024]{1,0:T(8,128)S(1)}, u32[]{:S(2)}, u32[]{:S(2)}) collective-permute-start(f32[64,1024]{1,0:T(8,128)S(1)} %copy-done.3), channel_id=1, source_target_pairs={{0,1},{1,0},{2,3},{3,2},{4,5},{5,4},{6,7},{7,6},{8,9},{9,8},{10,11... | collective-permute-start | bytes 786440 | tf_op jit(solution)/shard_map/grad_swap/ppermute | solution.py:952
  140.1 0.7 copy-start.4
  147.6 1.2 collective-permute-start.10
